TPU v7x, 32 devices: a whole 2x2x4 slice. The times are simulated.
32 devices in a mesh: neg: 8 (over z, y), rep: 4 (over x, core).
Axes of the slice: x: 2, y: 2, z: 4, core: 2. Of those that a mesh axis runs over, the one named last changes fastest.
Arguments:
- goal_states: bfloat16 [4, 64, 128, 512], P('rep', 'neg'), may hold values from -6 to 6
- premise_states: bfloat16 [4, 256, 128, 512], P('rep', 'neg'), may hold values from -6 to 6
- goal_ids: int32 [4, 64, 128], P('rep', 'neg'), may hold values from 0 to 31999, as said below
- premise_ids: int32 [4, 256, 128], P('rep', 'neg'), may hold values from 0 to 31999, as said below
- positives: int32 [4, 64], P('rep'), may hold values from 0 to 255
- depthwise_kernels: float32 [2, 3, 512], replicated, may hold values from -3.5 to 3.5
- block_norm_gains: float32 [2, 512], replicated, may hold values from 0.25 to 1.75
- pointwise_weights: bfloat16 [2, 512, 512], replicated, may hold values from -0.25 to 0.25
- head_weight: bfloat16 [512, 256], replicated, may hold values from -0.25 to 0.25
Outputs:
- goal_loss: float32 [4, 64], P('rep', 'neg')
- grad_depth: float32 [2, 3, 512], replicated
- grad_gain: float32 [2, 512], replicated
- grad_point: float32 [2, 512, 512], replicated
- grad_head: float32 [512, 256], replicated
Inputs may be any that keep to these rules, and one draw needn't show every extreme that they name: `goal_ids`: id 0 marks padding: a sequence's ids are nonzero on its first positions and 0 after them, with at least 16 nonzero ids. `premise_ids`: id 0 marks padding: a sequence's ids are nonzero on its first positions and 0 after them, with at least 16 nonzero ids.
All inputs are finite; a program needn't handle non-finite values.
Results may differ from a plain program's by a relative error of at most 0.022.
Values may be sent and summed in bfloat16 or wider, within the bound.
A program may use at most 192 MiB of HBM per device.

v0:
```python
import jax
import jax.numpy as jnp
from jax import lax
from jax.sharding import PartitionSpec as P

LOWER_DILATION = 4
UPPER_DILATION = 8


logit_scale = 20.0


def shift_down(values, dilation):
    return jnp.pad(values, ((0, 0), (dilation, 0), (0, 0)))[:, : values.shape[1]]


def shift_up(values, dilation):
    return jnp.pad(values, ((0, 0), (0, dilation), (0, 0)))[:, dilation:]


def depth_conv(inputs, kernel, dilation):
    return (
        kernel[0] * shift_down(inputs, dilation)
        + kernel[1] * inputs
        + kernel[2] * shift_up(inputs, dilation)
    )


def conv_block_forward(hidden, kernel, gain, weight, token_valid_mask, dilation):
    widened = hidden.astype(jnp.float32)
    inverse = lax.rsqrt(jnp.mean(widened * widened, axis=-1, keepdims=True) + 1e-06)
    normed = widened * inverse * gain * token_valid_mask
    mixed = depth_conv(normed, kernel, dilation).astype(jnp.bfloat16)
    count, length, width = hidden.shape
    pre_act = jnp.dot(
        mixed.reshape(count * length, width), weight, preferred_element_type=jnp.float32
    ).reshape(count, length, width)
    output = (widened + jax.nn.gelu(pre_act, approximate=True)).astype(jnp.bfloat16)
    return (output, (inverse, mixed, pre_act))


def conv_block_backward(
    upstream, hidden, saved, kernel, gain, weight, token_valid_mask, dilation, need_input
):
    inverse, mixed, pre_act = saved
    widened = hidden.astype(jnp.float32)
    normed = widened * inverse * gain * token_valid_mask
    ignored_value, gelu_back = jax.vjp(lambda value: jax.nn.gelu(value, approximate=True), pre_act)
    act_grad = gelu_back(upstream)[0].astype(jnp.bfloat16)
    count, length, width = hidden.shape
    flat_grad = act_grad.reshape(count * length, width)
    grad_weight = jnp.dot(
        mixed.reshape(count * length, width).T, flat_grad, preferred_element_type=jnp.float32
    )
    conv_grad = jnp.dot(flat_grad, weight.T, preferred_element_type=jnp.float32).reshape(
        count, length, width
    )
    grad_kernel = jnp.stack(
        [
            jnp.sum(shift_down(normed, dilation) * conv_grad, axis=(0, 1)),
            jnp.sum(normed * conv_grad, axis=(0, 1)),
            jnp.sum(shift_up(normed, dilation) * conv_grad, axis=(0, 1)),
        ]
    )
    normed_grad = (
        kernel[0] * shift_up(conv_grad, dilation)
        + kernel[1] * conv_grad
        + kernel[2] * shift_down(conv_grad, dilation)
    ) * token_valid_mask
    grad_gain = jnp.sum(normed_grad * widened * inverse, axis=(0, 1))
    input_grad = None
    if need_input:
        scaled = normed_grad * gain
        input_grad = (
            upstream
            + inverse * scaled
            - widened * inverse**3 * jnp.mean(scaled * widened, axis=-1, keepdims=True)
        )
    return (input_grad, grad_kernel, grad_gain, grad_weight)


def pool_forward(hidden, token_valid_mask, head_weight):
    widened = hidden.astype(jnp.float32)
    counts = jnp.sum(token_valid_mask, axis=1)
    pooled = (jnp.sum(widened * token_valid_mask, axis=1) / counts).astype(jnp.bfloat16)
    embedded = jnp.dot(pooled, head_weight, preferred_element_type=jnp.float32)
    magnitude = jnp.sqrt(jnp.sum(embedded * embedded, axis=-1, keepdims=True) + 1e-06)
    unit = embedded / magnitude
    return (unit.astype(jnp.bfloat16), (counts, pooled, unit, magnitude))


def pool_backward(unit_grad, saved, token_valid_mask, head_weight):
    counts, pooled, unit, magnitude = saved
    embed_grad = (
        (unit_grad - unit * jnp.sum(unit * unit_grad, axis=-1, keepdims=True)) / magnitude
    ).astype(jnp.bfloat16)
    grad_head = jnp.dot(pooled.T, embed_grad, preferred_element_type=jnp.float32)
    pooled_grad = jnp.dot(embed_grad, head_weight.T, preferred_element_type=jnp.float32)
    hidden_gradient = (pooled_grad / counts)[:, None, :] * token_valid_mask
    return (hidden_gradient, grad_head)


def local(
    goal_states,
    premise_states,
    goal_ids,
    premise_ids,
    positives,
    depthwise_kernels,
    block_norm_gains,
    pointwise_weights,
    head_weight,
):
    goal_count = goal_states.shape[1]
    token_states = jnp.concatenate([goal_states[0], premise_states[0]], axis=0)
    token_ids = jnp.concatenate([goal_ids[0], premise_ids[0]], axis=0)
    token_valid_mask = (token_ids != 0).astype(jnp.float32)[..., None]
    first_hidden, lower_residuals = conv_block_forward(
        token_states,
        depthwise_kernels[0],
        block_norm_gains[0],
        pointwise_weights[0],
        token_valid_mask,
        LOWER_DILATION,
    )
    second_hidden, upper_residuals = conv_block_forward(
        first_hidden,
        depthwise_kernels[1],
        block_norm_gains[1],
        pointwise_weights[1],
        token_valid_mask,
        UPPER_DILATION,
    )
    units, saved_pool = pool_forward(second_hidden, token_valid_mask, head_weight)
    goal_units = units[:goal_count]
    premise_units = units[goal_count:]
    group_positive = positives[0]
    position = lax.axis_index("neg")
    group_premises = lax.all_gather(premise_units, "neg", axis=0, tiled=True)
    own_positive = lax.dynamic_slice_in_dim(group_positive, position * goal_count, goal_count)
    scores = logit_scale * lax.dot_general(
        goal_units, group_premises, (((1,), (1,)), ((), ())), preferred_element_type=jnp.float32
    )
    expon = jnp.exp(scores)
    total = jnp.sum(expon, axis=1, keepdims=True)
    columns = jnp.arange(group_premises.shape[0], dtype=jnp.int32)
    onehot = (columns[None, :] == own_positive[:, None]).astype(jnp.float32)
    losses = jnp.log(total[:, 0]) - jnp.sum(scores * onehot, axis=1)
    score_grad = ((expon / total - onehot) / goal_count).astype(jnp.bfloat16)
    goal_grad = logit_scale * jnp.dot(
        score_grad, group_premises, preferred_element_type=jnp.float32
    )
    premise_grad = lax.psum_scatter(
        logit_scale
        * lax.dot_general(
            score_grad, goal_units, (((0,), (0,)), ((), ())), preferred_element_type=jnp.float32
        ),
        "neg",
        scatter_dimension=0,
        tiled=True,
    )
    unit_grad = jnp.concatenate([goal_grad, premise_grad], axis=0)
    hidden_gradient, grad_head = pool_backward(unit_grad, saved_pool, token_valid_mask, head_weight)
    lower_gradient, upper_kernel, upper_gain, upper_weight = conv_block_backward(
        hidden_gradient,
        first_hidden,
        upper_residuals,
        depthwise_kernels[1],
        block_norm_gains[1],
        pointwise_weights[1],
        token_valid_mask,
        UPPER_DILATION,
        True,
    )
    ignored_value, lower_kernel, lower_gain, lower_weight = conv_block_backward(
        lower_gradient,
        token_states,
        lower_residuals,
        depthwise_kernels[0],
        block_norm_gains[0],
        pointwise_weights[0],
        token_valid_mask,
        LOWER_DILATION,
        False,
    )
    grad_head, upper_kernel, upper_gain, upper_weight, lower_kernel, lower_gain, lower_weight = (
        lax.psum(
            (
                grad_head,
                upper_kernel,
                upper_gain,
                upper_weight,
                lower_kernel,
                lower_gain,
                lower_weight,
            ),
            ("neg", "rep"),
        )
    )
    return (
        losses[None, :],
        jnp.stack([lower_kernel, upper_kernel]),
        jnp.stack([lower_gain, upper_gain]),
        jnp.stack([lower_weight, upper_weight]),
        grad_head,
    )


def solution(mesh):
    placed = (
        P("rep", "neg", None, None),
        P("rep", "neg", None, None),
        P("rep", "neg", None),
        P("rep", "neg", None),
        P("rep", None),
        P(),
        P(),
        P(),
        P(),
    )
    return jax.shard_map(
        local,
        mesh=mesh,
        in_specs=placed,
        out_specs=(P("rep", "neg"), P(), P(), P(), P()),
        check_vma=False,
    )
```

profile of v0, /device:TPU:1, one launch (start us, length us, event | category | flops | bytes accessed | tf_op | source)
XLA Modules:
  0.0 360.2 jit_solution(12414875883324808904)
XLA Ops:
  8.8 3.6 fusion.24
  13.1 4.0 %fusion.26 = f32[40,128,512]{2,1,0:T(8,128)S(1)} fusion(f32[40,128]{1,0:T(8,128)S(1)} %fusion.54, f32[512]{0:T(512)S(1)} %bitcast.95, f32[40,128]{1,0:T(8,128)S(1)} %add_rsqrt_fusion.1, bf16[32,128,512]{2,1,0:T(8,128)(2,1)} %bitcast.69, bf16[8,128,512]{2,1,0:T(8,128)(2,1)} %bitcast.75), kind=kLoop, calls=%fused_computation.51 | loop fusion | flops 13107200 | bytes 15771648 | tf_op jit(solution)/shard_map/mul | solution.py:32
  17.1 5.3 %copy-done.2 = f32[40,128,512]{2,1,0:T(8,128)} copy-done((f32[40,128,512]{2,1,0:T(8,128)}, f32[40,128,512]{2,1,0:T(8,128)S(1)}, u32[]{:S(2)}) %copy-start.2) | copy-done | bytes 10485784
  22.4 3.8 %add_convert_fusion.1 = bf16[40,128,512]{2,1,0:T(8,128)(2,1)S(1)} fusion(f32[40,128,512]{2,1,0:T(8,128)S(1)} %fusion.26, f32[512]{0:T(512)S(1)} %bitcast.89, f32[512]{0:T(512)S(1)} %bitcast.91, f32[512]{0:T(512)S(1)} %bitcast.93), kind=kLoop, calls=%fused_computation.74 | loop fusion | flops 15728640 | bytes 15734784 | tf_op jit(solution)/shard_map/convert_element_type | solution.py:33
  26.2 8.3 %fusion.33 = (f32[40,128]{1,0:T(8,128)S(1)}, bf16[40,128,512]{2,1,0:T(8,128)(2,1)S(1)}, f32[40,128,512]{2,1,0:T(8,128)}) fusion(bf16[32,128,512]{2,1,0:T(8,128)(2,1)S(1)} %bitcast.71, bf16[8,128,512]{2,1,0:T(8,128)(2,1)S(1)} %bitcast.76, bf16[40,128,512]{2,1,0:T(8,128)(2,1)S(1)} %add_convert_fusion.1, bf16[2,512,512]{2,1,0:T(8,128)(2,1)S(1)} %copy-done.9), kind=kOutput, calls=%fused_computation.58 | convolution fusion | flops 2723671040 | bytes 26759168 | tf_op jit(solution)/shard_map/dot_general | solution.py:35
  34.6 1.7 fusion.35
  36.3 4.0 %copy-done.3 = f32[40,128,512]{2,1,0:T(8,128)} copy-done((f32[40,128,512]{2,1,0:T(8,128)}, f32[40,128,512]{2,1,0:T(8,128)S(1)}, u32[]{:S(2)}) %copy-start.3) | copy-done | bytes 10485784
  40.3 4.4 %add_convert_fusion = bf16[40,128,512]{2,1,0:T(8,128)(2,1)S(1)} fusion(f32[40,128,512]{2,1,0:T(8,128)S(1)} %fusion.35, f32[512]{0:T(512)S(1)} %bitcast.85, f32[512]{0:T(512)S(1)} %bitcast.87, f32[512]{0:T(512)S(1)} %bitcast.83), kind=kLoop, calls=%fused_computation.73 | loop fusion | flops 15728640 | bytes 15734784 | tf_op jit(solution)/shard_map/convert_element_type | solution.py:33
  44.7 8.2 %multiply_reduce_fusion.6 = (f32[40,512]{1,0:T(8,128)S(1)}, f32[40,128,512]{2,1,0:T(8,128)}) fusion(f32[40,128]{1,0:T(8,128)S(1)} %fusion.54, bf16[40,128,512]{2,1,0:T(8,128)(2,1)S(1)} %get-tuple-element.34, bf16[40,128,512]{2,1,0:T(8,128)(2,1)S(1)} %add_convert_fusion, bf16[2,512,512]{2,1,0:T(8,128)(2,1)S(1)} %copy-done.9), kind=kOutput, calls=%fused_computation.72 | convolution fusion | flops 2721034240 | bytes 21598208 | tf_op jit(solution)/shard_map/dot_general | solution.py:35
  53.5 25.6 %all_gather.3 = bf16[256,256]{1,0:T(8,128)(2,1)S(1)} all-gather(bf16[32,256]{1,0:T(8,128)(2,1)S(1)} %slice.111), channel_id=1, replica_groups=mesh['neg'=8,'rep'=4] {'neg'}, dimensions={0}, use_global_device_ids=true | all-gather | bytes 147456 | tf_op jit(solution)/shard_map/all_gather | solution.py:139
  81.5 65.5 %reduce-scatter.2.cloned.1.call-done = f32[32,256]{1,0:T(8,128)} async-done(((f32[256,256]{1,0:T(8,128)}), f32[32,256]{1,0:T(8,128)}) %reduce-scatter.2.cloned.1.call-update) | async-done | bytes 32784 | tf_op jit(solution)/shard_map/reduce_scatter | solution.py:153
  149.0 9.4 %fusion.23 = bf16[40,128,512]{2,1,0:T(8,128)(2,1)S(1)} fusion(f32[40,128,512]{2,1,0:T(8,128)} %get-tuple-element.47, f32[40,512]{1,0:T(8,128)S(1)} %convolution_divide_fusion, f32[40,128]{1,0:T(8,128)S(1)} %fusion.54), kind=kLoop, calls=%fused_computation.48 | loop fusion | flops 55050240 | bytes 15831040 | tf_op jit(solution)/shard_map/convert_element_type | solution.py:49
  158.4 3.9 %convolution_bitcast_fusion = f32[1,512,512]{2,1,0:T(8,128)} fusion(bf16[40,128,512]{2,1,0:T(8,128)(2,1)S(1)} %bitcast.73, bf16[40,128,512]{2,1,0:T(8,128)(2,1)S(1)} %fusion.23), kind=kOutput, calls=%fused_computation.78 | convolution fusion | flops 2684354560 | bytes 11534336 | tf_op jit(solution)/shard_map/dot_general | solution.py:52
  162.3 5.4 %fusion.42 = f32[40,128,512]{2,1,0:T(8,128)} fusion(bf16[40,128,512]{2,1,0:T(8,128)(2,1)S(1)} %fusion.23, bf16[2,512,512]{2,1,0:T(8,128)(2,1)S(1)} %copy-done.10), kind=kOutput, calls=%fused_computation.84 | convolution fusion | flops 2684354560 | bytes 16252928 | tf_op jit(solution)/shard_map/dot_general | solution.py:55
  167.8 18.8 %multiply_reduce_fusion.2 = (f32[512]{0:T(512)S(1)}, f32[512]{0:T(512)S(1)}, f32[512]{0:T(512)S(1)}, f32[40,128]{1,0:T(8,128)S(1)}, f32[512]{0:T(512)S(1)}, /*index=5*/f32[40,128,512]{2,1,0:T(8,128)}) fusion(f32[40,128,512]{2,1,0:T(8,128)} %fusion.42, f32[40,128,512]{2,1,0:T(8,128)S(1)} %bitcast.65, f32[40,128]{1,0:T(8,128)S(1)} %fusion.54, ...), kind=kLoop, calls=%fused_computation.68 | loop fusion | flops 57664512 | bytes 36777984 | tf_op jit(solution)/shard_map/reduce_sum | solution.py:60
  186.6 12.0 %fusion.16 = bf16[40,128,512]{2,1,0:T(8,128)(2,1)S(1)} fusion(f32[40,128,512]{2,1,0:T(8,128)} %get-tuple-element.45, bf16[40,128,512]{2,1,0:T(8,128)(2,1)S(1)} %bitcast.67, f32[40,128,512]{2,1,0:T(8,128)} %get-tuple-element.32, f32[40,128]{1,0:T(8,128)S(1)} %broadcast_multiply_fusion, f32[40,128]{1,0:T(8,128)S(1)} %get-tuple-element.35, ...), kind=kLoop, calls=%fused_computation.41 | loop fusion | flops 73400320 | bytes 31623168 | tf_op jit(solution)/shard_map/convert_element_type | solution.py:49
  198.6 6.4 %convolution_bitcast_fusion.1 = f32[1,512,512]{2,1,0:T(8,128)} fusion(bf16[40,128,512]{2,1,0:T(8,128)(2,1)} %copy-done.6, bf16[40,128,512]{2,1,0:T(8,128)(2,1)S(1)} %fusion.16), kind=kOutput, calls=%fused_computation.79 | convolution fusion | flops 2684354560 | bytes 11534336 | tf_op jit(solution)/shard_map/dot_general | solution.py:52
  205.0 5.5 %fusion.46 = f32[40,128,512]{2,1,0:T(8,128)} fusion(bf16[40,128,512]{2,1,0:T(8,128)(2,1)S(1)} %fusion.16, bf16[2,512,512]{2,1,0:T(8,128)(2,1)S(1)} %copy-done.11), kind=kOutput, calls=%fused_computation.88 | convolution fusion | flops 2684354560 | bytes 16252928 | tf_op jit(solution)/shard_map/dot_general | solution.py:55
  210.5 1.1 fusion.58
  211.6 27.2 %fusion.41 = (f32[512]{0:T(512)S(1)}, f32[512]{0:T(512)S(1)}, f32[512]{0:T(512)S(1)}, f32[512]{0:T(512)S(1)}) fusion(f32[40,128,512]{2,1,0:T(8,128)} %fusion.46, f32[512]{0:T(512)S(1)} %bitcast.90, f32[512]{0:T(512)S(1)} %bitcast.92, f32[40,128]{1,0:T(8,128)S(1)} %fusion.54, f32[40,128]{1,0:T(8,128)S(1)} %add_rsqrt_fusion.1, f32[512]{0:T(512)S(1)} %bitcast.94, ...), kind=kLoop, calls=%fused_computation.75 | loop fusion | flops 52426752 | bytes 26271744 | tf_op jit(solution)/shard_map/reduce_sum | solution.py:70
  238.9 42.1 %all-reduce.8 = (f32[1,3,512]{2,1,0:T(4,128)S(1)}, f32[1,3,512]{2,1,0:T(4,128)S(1)}, f32[1,512]{1,0:T(1,128)S(1)}, f32[1,512]{1,0:T(1,128)S(1)}) all-reduce(f32[1,3,512]{2,1,0:T(4,128)S(1)} %get-tuple-element.52, f32[1,3,512]{2,1,0:T(4,128)S(1)} %get-tuple-element.51, ...), channel_id=1, replica_groups=mesh['neg'=8,'rep'=4] {'neg','rep'}, use_global_device_ids=true, to_apply=%region_17.18 | all-reduce | flops 4096 | bytes 32768 | tf_op jit(solution)/shard_map/psum | solution.py:187
  282.3 66.2 %all-reduce.12.cloned.1.call-done = (f32[1,512,512]{2,1,0:T(8,128)}, f32[1,512,512]{2,1,0:T(8,128)}, f32[512,256]{1,0:T(8,128)}) async-done(((f32[1,512,512]{2,1,0:T(8,128)}, f32[1,512,512]{2,1,0:T(8,128)}, f32[512,256]{1,0:T(8,128)}), (f32[1,512,512]{2,1,0:T(8,128)}, f32[1,512,512]{2,1,0:T(8,128)}, f32[512,256]{1,0:T(8,128)})) %all-reduce.12.cloned.1.call-update) | async-done | bytes 2621456 | tf_op jit(solution)/shard_map/psum | solution.py:187
  348.5 3.0 pad_maximum_fusion.1
  351.5 1.9 copy.24
  (73 shorter events, 8.5 us)
Async XLA Ops:
  7.2 45.9 %copy-start = (bf16[512,256]{1,0:T(8,128)(2,1)S(1)}, bf16[512,256]{1,0:T(8,128)(2,1)}, u32[]{:S(2)}) copy-start(bf16[512,256]{1,0:T(8,128)(2,1)} %param.17) | copy-start | bytes 786436
  7.2 139.9 %reduce-scatter.2.cloned.1.call-start = ((), (), s32[]{:S(2)}) async-start(), calls=%async_computation.1 | async-start | bytes 294912 | tf_op jit(solution)/shard_map/reduce_scatter | solution.py:153
  17.1 5.3 %copy-start.2 = (f32[40,128,512]{2,1,0:T(8,128)}, f32[40,128,512]{2,1,0:T(8,128)S(1)}, u32[]{:S(2)}) copy-start(f32[40,128,512]{2,1,0:T(8,128)S(1)} %fusion.26) | copy-start | bytes 31457284
  17.1 9.1 %copy-start.5 = (bf16[1,32,128,512]{3,2,1,0:T(8,128)(2,1)S(1)}, bf16[1,32,128,512]{3,2,1,0:T(8,128)(2,1)}, u32[]{:S(2)}) copy-start(bf16[1,32,128,512]{3,2,1,0:T(8,128)(2,1)} %param.10) | copy-start | bytes 12582916
  17.1 9.1 %copy-start.8 = (bf16[1,8,128,512]{3,2,1,0:T(8,128)(2,1)S(1)}, bf16[1,8,128,512]{3,2,1,0:T(8,128)(2,1)}, u32[]{:S(2)}) copy-start(bf16[1,8,128,512]{3,2,1,0:T(8,128)(2,1)} %param.9) | copy-start | bytes 3145732
  17.1 9.1 %copy-start.9 = (bf16[2,512,512]{2,1,0:T(8,128)(2,1)S(1)}, bf16[2,512,512]{2,1,0:T(8,128)(2,1)}, u32[]{:S(2)}) copy-start(bf16[2,512,512]{2,1,0:T(8,128)(2,1)} %param.16) | copy-start | bytes 3145732
  26.2 8.3 %copy-start.6 = (bf16[40,128,512]{2,1,0:T(8,128)(2,1)}, bf16[40,128,512]{2,1,0:T(8,128)(2,1)S(1)}, u32[]{:S(2)}) copy-start(bf16[40,128,512]{2,1,0:T(8,128)(2,1)S(1)} %add_convert_fusion.1) | copy-start | bytes 15728644
  34.6 10.1 %copy-start.4 = (bf16[40,128,512]{2,1,0:T(8,128)(2,1)}, bf16[40,128,512]{2,1,0:T(8,128)(2,1)S(1)}, u32[]{:S(2)}) copy-start(bf16[40,128,512]{2,1,0:T(8,128)(2,1)S(1)} %get-tuple-element.34) | copy-start | bytes 15728644
  36.3 4.0 %copy-start.3 = (f32[40,128,512]{2,1,0:T(8,128)}, f32[40,128,512]{2,1,0:T(8,128)S(1)}, u32[]{:S(2)}) copy-start(f32[40,128,512]{2,1,0:T(8,128)S(1)} %fusion.35) | copy-start | bytes 31457284
  44.7 8.3 %copy-start.7 = (bf16[40,128,512]{2,1,0:T(8,128)(2,1)}, bf16[40,128,512]{2,1,0:T(8,128)(2,1)S(1)}, u32[]{:S(2)}) copy-start(bf16[40,128,512]{2,1,0:T(8,128)(2,1)S(1)} %add_convert_fusion) | copy-start | bytes 15728644
  44.7 8.3 %copy-start.12 = (s32[1,32,128]{2,1,0:T(8,128)S(1)}, s32[1,32,128]{2,1,0:T(8,128)}, u32[]{:S(2)}) copy-start(s32[1,32,128]{2,1,0:T(8,128)} %param.12) | copy-start | bytes 49156
  44.7 8.3 %copy-start.14 = (s32[1,8,128]{2,1,0:T(8,128)S(1)}, s32[1,8,128]{2,1,0:T(8,128)}, u32[]{:S(2)}) copy-start(s32[1,8,128]{2,1,0:T(8,128)} %param.11) | copy-start | bytes 12292
  44.7 34.4 %copy-start.15 = (s32[1,64]{1,0:T(1,128)S(1)}, s32[1,64]{1,0:T(1,128)}, u32[]{:S(2)}) copy-start(s32[1,64]{1,0:T(1,128)} %param.13) | copy-start | bytes 772
  53.0 105.4 %slice-start.5 = ((s8[5242880]{0:T(1024)(128)(4,1)}), s8[1048576]{0:T(1024)(128)(4,1)S(1)}, s32[]{:S(2)}) async-start(s8[5242880]{0:T(1024)(128)(4,1)} %bitcast.72), calls=%async_computation.8 | async-start | bytes 2097152
  80.6 267.9 %all-reduce.12.cloned.1.call-start = ((), (), s32[]{:S(2)}) async-start(), calls=%async_computation.2 | async-start | bytes 5242880 | tf_op jit(solution)/shard_map/psum | solution.py:187
  149.0 9.4 %slice-start.6 = ((s8[5242880]{0:T(1024)(128)(4,1)}), s8[4194304]{0:T(1024)(128)(4,1)S(1)}, s32[]{:S(2)}) async-start(s8[5242880]{0:T(1024)(128)(4,1)} %bitcast.72), calls=%async_computation.9 | async-start | bytes 8388608
  158.4 9.3 %slice-start = ((s8[10485760]{0:T(1024)(128)(4,1)}), s8[4194304]{0:T(1024)(128)(4,1)S(1)}, s32[]{:S(2)}) async-start(s8[10485760]{0:T(1024)(128)(4,1)} %bitcast.64), calls=%async_computation.3 | async-start | bytes 8388608
  158.4 9.3 %slice-start.1 = ((s8[10485760]{0:T(1024)(128)(4,1)}), s8[4194304]{0:T(1024)(128)(4,1)S(1)}, s32[]{:S(2)}) async-start(s8[10485760]{0:T(1024)(128)(4,1)} %bitcast.64), calls=%async_computation.4 | async-start | bytes 8388608
  158.4 9.3 %slice-start.3 = ((s8[5242880]{0:T(1024)(128)(4,1)}), s8[4194304]{0:T(1024)(128)(4,1)S(1)}, s32[]{:S(2)}) async-start(s8[5242880]{0:T(1024)(128)(4,1)} %bitcast.66), calls=%async_computation.6 | async-start | bytes 8388608
  162.3 5.4 %slice-start.2 = ((s8[10485760]{0:T(1024)(128)(4,1)}), s8[2097152]{0:T(1024)(128)(4,1)S(1)}, s32[]{:S(2)}) async-start(s8[10485760]{0:T(1024)(128)(4,1)} %bitcast.64), calls=%async_computation.5 | async-start | bytes 4194304
  162.3 5.4 %slice-start.4 = ((s8[5242880]{0:T(1024)(128)(4,1)}), s8[1048576]{0:T(1024)(128)(4,1)S(1)}, s32[]{:S(2)}) async-start(s8[5242880]{0:T(1024)(128)(4,1)} %bitcast.66), calls=%async_computation.7 | async-start | bytes 2097152
  198.6 6.5 %copy-start.11 = (bf16[2,512,512]{2,1,0:T(8,128)(2,1)S(1)}, bf16[2,512,512]{2,1,0:T(8,128)(2,1)}, u32[]{:S(2)}) copy-start(bf16[2,512,512]{2,1,0:T(8,128)(2,1)} %param.16) | copy-start | bytes 3145732
  205.0 5.5 %copy-start.13 = (f32[32,256]{1,0:T(8,128)S(1)}, f32[32,256]{1,0:T(8,128)}, u32[]{:S(2)}) copy-start(f32[32,256]{1,0:T(8,128)} %reduce-scatter.2.cloned.1.call-done) | copy-start | bytes 98308
  211.6 141.7 %copy-start.1 = (bf16[512,256]{1,0:T(8,128)(2,1)S(1)}, bf16[512,256]{1,0:T(8,128)(2,1)}, u32[]{:S(2)}) copy-start(bf16[512,256]{1,0:T(8,128)(2,1)} %param.17) | copy-start | bytes 786436
  (1 other events, 3.9 us)
Sparse Core Ops, SparseCore 0:
  80.7 66.3 reduce-scatter.1
  211.8 136.6 all-reduce.11
where the time goes:
time: 363 us; the launch traced here: 360 us
  waiting for transfers between devices  132 us (36%)
  other arithmetic  91 us (25%)
  blocking collectives  67.8 us (19%)
  matrix products  41.6 us (11%)
  between operations  14.4 us (4%)
  local copies, waits for them, and re-layouts  13.4 us (4%)
    psum x1, waiting for transfers between devices, local(): lax.psum((grad_head, upper_kernel, upper_gain, upper_weight, lower_kernel...  66.2 us
    reduce_scatter x1, waiting for transfers between devices, local(): lax.psum_scatter(logit_scale * lax.dot_general(score_grad, goal_units, ((...  65.5 us
    psum x1, blocking collectives, local(): lax.psum((grad_head, upper_kernel, upper_gain, upper_weight, lower_kernel...  42.1 us
    reduce_sum x1, other arithmetic, conv_block_backward(): grad_gain = jnp.sum(normed_grad * widened * inverse, axis=(0, 1))  27.2 us
    all_gather x1, blocking collectives, local(): group_premises = lax.all_gather(premise_units, 'neg', axis=0, tiled=True)  25.6 us
    convert_element_type x2, other arithmetic, conv_block_backward(): act_grad = gelu_back(upstream)[0].astype(jnp.bfloat16)  21.4 us
    reduce_sum x1, other arithmetic, conv_block_backward(): jnp.sum(shift_down(normed, dilation) * conv_grad, axis=(0, 1))  18.8 us
    dot_general x2, matrix products, conv_block_forward(): jnp.dot(mixed.reshape(count * length, width), weight, preferred_element_t...  16.5 us
  transfers between devices with their start and end apart: 2, of which 2 were waited for; matrix products, arithmetic and copies ran while one was open for 8% of the time, Pallas kernels for 0%

commit v1 on v0

v1 whole, which is shorter than its diff:
```python
import functools

import jax
import jax.numpy as jnp
from jax import lax
from jax.experimental import pallas as pl
from jax.experimental.pallas import tpu as pltpu
from jax.sharding import PartitionSpec as P

LOWER_DILATION = 4
UPPER_DILATION = 8
LOGIT_SCALE = 20.0
GELU_C = 0.7978845608028654
GELU_A = 0.044715
SEQS = 4
MESH = pl.DeviceIdType.MESH
VMEM_LIMIT = 56 * 1024 * 1024


def shift_down(values, dilation):
    zeros = jnp.zeros_like(values[:, :dilation])
    return jnp.concatenate([zeros, values[:, : values.shape[1] - dilation]], axis=1)


def shift_up(values, dilation):
    zeros = jnp.zeros_like(values[:, :dilation])
    return jnp.concatenate([values[:, dilation:], zeros], axis=1)


def gelu_and_slope(value):
    square = value * value
    half = 0.5 + 0.5 * jnp.tanh(value * (GELU_C + (GELU_C * GELU_A) * square))
    slope = half + value * (half - half * half) * (2.0 * GELU_C + (6.0 * GELU_C * GELU_A) * square)
    return value * half, slope


def length_mask(lens_ref, step, length):
    place = lax.broadcasted_iota(jnp.int32, (length, 1), 0)
    return jnp.stack(
        [(place < lens_ref[step * SEQS + s]).astype(jnp.float32) for s in range(SEQS)]
    )


def forward_kernel(
    goal_steps, lens_ref, goal_ref, prem_ref, kern_ref, gain_ref, weight_ref,
    n0_ref, m0_ref, d0_ref, n1_ref, m1_ref, d1_ref, inv_ref, pool_ref,
):
    step = pl.program_id(0)
    count, length, width = prem_ref.shape
    states = jnp.where(step < goal_steps, goal_ref[...], prem_ref[...])
    mask = length_mask(lens_ref, step, length)

    def block(hidden, b, dilation, n_ref, m_ref, d_ref):
        inverse = lax.rsqrt(jnp.mean(hidden * hidden, axis=-1, keepdims=True) + 1e-06) * mask
        unscaled = hidden * inverse
        n_ref[...] = unscaled.astype(jnp.bfloat16)
        taps = kern_ref[b] * gain_ref[b][None, :]
        mixed = (
            taps[0] * shift_down(unscaled, dilation)
            + taps[1] * unscaled
            + taps[2] * shift_up(unscaled, dilation)
        ).astype(jnp.bfloat16)
        m_ref[...] = mixed
        pre_act = jnp.dot(
            mixed.reshape(count * length, width), weight_ref[b], preferred_element_type=jnp.float32
        ).reshape(count, length, width)
        act, slope = gelu_and_slope(pre_act)
        d_ref[...] = slope.astype(jnp.bfloat16)
        return (hidden + act).astype(jnp.bfloat16), inverse

    first, _ = block(states.astype(jnp.float32), 0, LOWER_DILATION, n0_ref, m0_ref, d0_ref)
    second, inverse = block(first.astype(jnp.float32), 1, UPPER_DILATION, n1_ref, m1_ref, d1_ref)
    inv_ref[...] = jnp.broadcast_to(inverse, inv_ref.shape)
    row = lax.broadcasted_iota(jnp.int32, (8, count * length), 0)
    col = lax.broadcasted_iota(jnp.int32, (8, count * length), 1)
    picks = jnp.zeros((8, count * length), jnp.float32)
    for s in range(SEQS):
        own = (row == s) & (col >= s * length) & (col < s * length + lens_ref[step * SEQS + s])
        picks = jnp.where(own, 1.0, picks)
    pool_ref[...] = jnp.dot(
        picks.astype(jnp.bfloat16),
        second.reshape(count * length, width),
        preferred_element_type=jnp.float32,
    )[None]


def run_forward(lens, goals, premises, kernels, gains, weights):
    goal_count, length, width = goals.shape
    goal_steps = goal_count // SEQS
    total = goal_count + premises.shape[0]
    steps = total // SEQS
    block = pl.BlockSpec((SEQS, length, width), lambda i, lens: (i, 0, 0))
    whole = lambda shape: pl.BlockSpec(shape, lambda i, lens: (0,) * len(shape))
    state = jax.ShapeDtypeStruct((total, length, width), jnp.bfloat16)
    return pl.pallas_call(
        functools.partial(forward_kernel, goal_steps),
        grid_spec=pltpu.PrefetchScalarGridSpec(
            num_scalar_prefetch=1,
            grid=(steps,),
            in_specs=[
                pl.BlockSpec(
                    (SEQS, length, width), lambda i, lens: (jnp.minimum(i, goal_steps - 1), 0, 0)
                ),
                pl.BlockSpec(
                    (SEQS, length, width), lambda i, lens: (jnp.maximum(i - goal_steps, 0), 0, 0)
                ),
                whole(kernels.shape),
                whole(gains.shape),
                whole(weights.shape),
            ],
            out_specs=[block] * 6
            + [
                pl.BlockSpec((SEQS, length, 128), lambda i, lens: (i, 0, 0)),
                pl.BlockSpec((1, 8, width), lambda i, lens: (i, 0, 0)),
            ],
        ),
        out_shape=[state] * 6
        + [
            jax.ShapeDtypeStruct((total, length, 128), jnp.float32),
            jax.ShapeDtypeStruct((steps, 8, width), jnp.float32),
        ],
        compiler_params=pltpu.CompilerParams(vmem_limit_bytes=VMEM_LIMIT),
    )(lens, goals, premises, kernels, gains, weights)


def contrast_kernel(
    n_neg, goal_count, pooled_ref, lens_ref, head_ref, positive_ref,
    loss_ref, pooled_grad_ref, head_grad_ref,
    units_ref, loss_all, goal_all, prem_all, send_sem, recv_sem,
):
    me = lax.axis_index("neg")
    barrier = pltpu.get_barrier_semaphore()

    @pl.loop(1, n_neg)
    def _(k):
        pl.semaphore_signal(
            barrier, inc=1, device_id={"neg": lax.rem(me + k, n_neg)}, device_id_type=MESH
        )

    rows = pooled_ref.shape[0]
    lens = lens_ref[...]
    pooled = (pooled_ref[...] / lens).astype(jnp.bfloat16)
    head = head_ref[...]
    embedded = jnp.dot(pooled, head, preferred_element_type=jnp.float32)
    magnitude = jnp.sqrt(jnp.sum(embedded * embedded, axis=-1, keepdims=True) + 1e-06)
    unit = embedded / magnitude
    units_ref[me] = unit.astype(jnp.bfloat16)
    pl.semaphore_wait(barrier, n_neg - 1)

    def copy_to(k):
        peer = lax.rem(me + k, n_neg)
        return pltpu.make_async_remote_copy(
            src_ref=units_ref.at[me],
            dst_ref=units_ref.at[me],
            send_sem=send_sem.at[k],
            recv_sem=recv_sem.at[me],
            device_id={"neg": peer},
            device_id_type=MESH,
        )

    @pl.loop(1, n_neg)
    def _(k):
        copy_to(k).start()

    @pl.loop(1, n_neg)
    def _(k):
        source = lax.rem(me + k, n_neg)
        pltpu.make_async_remote_copy(
            src_ref=units_ref.at[source],
            dst_ref=units_ref.at[source],
            send_sem=send_sem.at[k],
            recv_sem=recv_sem.at[source],
            device_id={"neg": source},
            device_id_type=MESH,
        ).wait_recv()

    everyone = units_ref[...].astype(jnp.float32)
    width = everyone.shape[-1]
    prem_count = rows - 2 * goal_count
    goals = everyone[:, :goal_count].reshape(n_neg * goal_count, width).astype(jnp.bfloat16)
    premises = everyone[:, 2 * goal_count :].reshape(n_neg * prem_count, width).astype(jnp.bfloat16)
    scores = LOGIT_SCALE * lax.dot_general(
        goals, premises, (((1,), (1,)), ((), ())), preferred_element_type=jnp.float32
    )
    expon = jnp.exp(scores)
    total = jnp.sum(expon, axis=1, keepdims=True)
    columns = lax.broadcasted_iota(jnp.int32, scores.shape, 1)
    onehot = (columns == positive_ref[...]).astype(jnp.float32)
    loss = jnp.log(total) - jnp.sum(scores * onehot, axis=1, keepdims=True)
    loss_all[...] = jnp.broadcast_to(loss, loss_all.shape)
    score_grad = ((expon / total - onehot) / goal_count).astype(jnp.bfloat16)
    goal_all[...] = LOGIT_SCALE * jnp.dot(score_grad, premises, preferred_element_type=jnp.float32)
    prem_all[...] = LOGIT_SCALE * lax.dot_general(
        score_grad, goals, (((0,), (0,)), ((), ())), preferred_element_type=jnp.float32
    )
    own_goals = pl.ds(pl.multiple_of(me * goal_count, goal_count), goal_count)
    own_prems = pl.ds(pl.multiple_of(me * prem_count, prem_count), prem_count)
    loss_ref[...] = loss_all[own_goals, :]
    own_goal_grad = goal_all[own_goals, :]
    unit_grad = jnp.concatenate(
        [own_goal_grad, jnp.zeros_like(own_goal_grad), prem_all[own_prems, :]], axis=0
    )
    embed_grad = (
        (unit_grad - unit * jnp.sum(unit * unit_grad, axis=-1, keepdims=True)) / magnitude
    ).astype(jnp.bfloat16)
    head_grad_ref[...] = lax.dot_general(
        pooled, embed_grad, (((0,), (0,)), ((), ())), preferred_element_type=jnp.float32
    )
    pooled_grad = lax.dot_general(
        embed_grad, head, (((1,), (1,)), ((), ())), preferred_element_type=jnp.float32
    )
    pooled_grad_ref[...] = pooled_grad / lens

    @pl.loop(1, n_neg)
    def _(k):
        copy_to(k).wait_send()


def run_contrast(n_neg, goal_count, pooled, lens, head, positives):
    rows, width = pooled.shape
    embed = head.shape[1]
    prem_count = rows - 2 * goal_count
    vmem = pl.BlockSpec(memory_space=pltpu.VMEM)
    return pl.pallas_call(
        functools.partial(contrast_kernel, n_neg, goal_count),
        out_shape=[
            jax.ShapeDtypeStruct((goal_count, 128), jnp.float32),
            jax.ShapeDtypeStruct((rows, width), jnp.float32),
            jax.ShapeDtypeStruct((width, embed), jnp.float32),
        ],
        in_specs=[vmem] * 4,
        out_specs=[vmem] * 3,
        scratch_shapes=[
            pltpu.VMEM((n_neg, rows, embed), jnp.bfloat16),
            pltpu.VMEM((n_neg * goal_count, 128), jnp.float32),
            pltpu.VMEM((n_neg * goal_count, embed), jnp.float32),
            pltpu.VMEM((n_neg * prem_count, embed), jnp.float32),
            pltpu.SemaphoreType.DMA((n_neg,)),
            pltpu.SemaphoreType.DMA((n_neg,)),
        ],
        compiler_params=pltpu.CompilerParams(
            collective_id=0, has_side_effects=True, vmem_limit_bytes=VMEM_LIMIT
        ),
    )(pooled, lens, head, positives)


def backward_kernel(
    lens_ref, n0_ref, m0_ref, d0_ref, n1_ref, m1_ref, d1_ref, inv_ref, up_ref,
    kern_ref, gain_ref, weight_ref,
    point_ref, small_ref, sums_ref,
):
    step = pl.program_id(0)
    count, length, width = n0_ref.shape
    tokens = count * length

    @pl.when(step == 0)
    def _():
        point_ref[...] = jnp.zeros_like(point_ref)
        sums_ref[...] = jnp.zeros_like(sums_ref)

    def fold(values):
        return jnp.sum(values.reshape(tokens // 8, 8, width), axis=0)

    def block(upstream, b, dilation, m_ref, d_ref, unscaled, need_input):
        act_grad = (upstream * d_ref[...].astype(jnp.float32)).astype(jnp.bfloat16)
        flat = act_grad.reshape(tokens, width)
        point_ref[b] += lax.dot_general(
            m_ref[...].reshape(tokens, width),
            flat,
            (((0,), (0,)), ((), ())),
            preferred_element_type=jnp.float32,
        )
        conv = lax.dot_general(
            flat, weight_ref[b], (((1,), (1,)), ((), ())), preferred_element_type=jnp.float32
        ).reshape(count, length, width)
        above = shift_up(conv, dilation)
        below = shift_down(conv, dilation)
        sums_ref[b, 0] += fold(above * unscaled)
        sums_ref[b, 1] += fold(conv * unscaled)
        sums_ref[b, 2] += fold(below * unscaled)
        if not need_input:
            return None
        taps = kern_ref[b] * gain_ref[b][None, :]
        scaled = taps[0] * above + taps[1] * conv + taps[2] * below
        mean = jnp.mean(scaled * unscaled, axis=-1, keepdims=True)
        inverse = inv_ref[:, :, :1]
        return upstream + inverse * (scaled - unscaled * mean)

    mask = length_mask(lens_ref, step, length)
    upstream = up_ref[...] * mask
    lower = block(
        upstream, 1, UPPER_DILATION, m1_ref, d1_ref, n1_ref[...].astype(jnp.float32), True
    )
    block(lower, 0, LOWER_DILATION, m0_ref, d0_ref, n0_ref[...].astype(jnp.float32), False)

    @pl.when(step == pl.num_programs(0) - 1)
    def _():
        rows = []
        for b in range(2):
            plain = jnp.sum(sums_ref[b], axis=1)
            rows.append(plain * gain_ref[b][None, :])
            rows.append(jnp.sum(plain * kern_ref[b], axis=0, keepdims=True))
        small_ref[...] = jnp.concatenate([rows[0], rows[2], rows[1], rows[3]], axis=0)


def run_backward(lens, saved, pooled_grad, kernels, gains, weights):
    total, length, width = saved[0].shape
    steps = total // SEQS
    block = pl.BlockSpec((SEQS, length, width), lambda i, lens: (i, 0, 0))
    whole = lambda shape: pl.BlockSpec(shape, lambda i, lens: (0,) * len(shape))
    return pl.pallas_call(
        backward_kernel,
        grid_spec=pltpu.PrefetchScalarGridSpec(
            num_scalar_prefetch=1,
            grid=(steps,),
            in_specs=[block] * 6
            + [
                pl.BlockSpec((SEQS, length, 128), lambda i, lens: (i, 0, 0)),
                pl.BlockSpec((SEQS, 1, width), lambda i, lens: (i, 0, 0)),
                whole(kernels.shape),
                whole(gains.shape),
                whole(weights.shape),
            ],
            out_specs=[whole(weights.shape), whole((8, width))],
            scratch_shapes=[pltpu.VMEM((2, 3, 8, width), jnp.float32)],
        ),
        out_shape=[
            jax.ShapeDtypeStruct(weights.shape, jnp.float32),
            jax.ShapeDtypeStruct((8, width), jnp.float32),
        ],
        compiler_params=pltpu.CompilerParams(vmem_limit_bytes=VMEM_LIMIT),
    )(lens, *saved, pooled_grad, kernels, gains, weights)


def reduce_kernel(
    n_neg, n_rep, point_ref, head_ref, small_ref,
    point_out, head_out, small_out,
    mine_ref, pair_ref, slots_ref, full_ref,
    pair_send, pair_recv, send_sem, recv_sem, send2_sem, recv2_sem, last_send, last_recv,
):
    neg = lax.axis_index("neg")
    rep = lax.axis_index("rep")
    half_rep = n_rep // 2
    chips = n_neg * half_rep
    core = lax.rem(rep, 2)
    other = 1 - core
    me = neg * half_rep + rep // 2
    twin = {"neg": neg, "rep": rep + 1 - 2 * core}

    def device_of(chip):
        return {"neg": chip // half_rep, "rep": 2 * lax.rem(chip, half_rep) + core}

    barrier = pltpu.get_barrier_semaphore()
    pl.semaphore_signal(barrier, inc=1, device_id=twin, device_id_type=MESH)

    @pl.loop(1, chips)
    def _(k):
        pl.semaphore_signal(
            barrier, inc=1, device_id=device_of(lax.rem(me + k, chips)), device_id_type=MESH
        )

    width = point_ref.shape[-1]
    cols = width // 2
    point_rows = 2 * width
    head_rows = head_ref.shape[0] // 2
    small_row = point_rows + head_rows
    total = mine_ref.shape[1]
    share = total // chips
    for h in range(2):
        side = slice(h * cols, (h + 1) * cols)
        for b in range(2):
            mine_ref[h, b * width : (b + 1) * width] = point_ref[b, :, side].astype(jnp.bfloat16)
        mine_ref[h, point_rows:small_row] = head_ref[
            h * head_rows : (h + 1) * head_rows, :
        ].astype(jnp.bfloat16)
        mine_ref[h, small_row:] = jnp.concatenate(
            [small_ref[:, side], jnp.zeros((total - small_row - 8, cols), jnp.float32)], axis=0
        ).astype(jnp.bfloat16)
    pl.semaphore_wait(barrier, chips)

    pair = pltpu.make_async_remote_copy(
        src_ref=mine_ref.at[other],
        dst_ref=pair_ref,
        send_sem=pair_send,
        recv_sem=pair_recv,
        device_id=twin,
        device_id_type=MESH,
    )
    pair.start()
    pair.wait_recv()
    mine_ref[core] = (
        mine_ref[core].astype(jnp.float32) + pair_ref[...].astype(jnp.float32)
    ).astype(jnp.bfloat16)

    def rows_of(chip):
        return pl.ds(pl.multiple_of(chip * share, 16), share)

    def scatter(k):
        chip = lax.rem(me + k, chips)
        return pltpu.make_async_remote_copy(
            src_ref=mine_ref.at[core, rows_of(chip)],
            dst_ref=slots_ref.at[me],
            send_sem=send_sem.at[k],
            recv_sem=recv_sem.at[me],
            device_id=device_of(chip),
            device_id_type=MESH,
        )

    def scattered(k):
        chip = lax.rem(me + k, chips)
        return pltpu.make_async_remote_copy(
            src_ref=slots_ref.at[chip],
            dst_ref=slots_ref.at[chip],
            send_sem=send_sem.at[k],
            recv_sem=recv_sem.at[chip],
            device_id=device_of(chip),
            device_id_type=MESH,
        )

    @pl.loop(1, chips)
    def _(k):
        scatter(k).start()

    slots_ref[me] = mine_ref[core, rows_of(me)]

    @pl.loop(1, chips)
    def _(k):
        scattered(k).wait_recv()

    reduced = lax.fori_loop(
        0,
        chips,
        lambda c, acc: acc + slots_ref[c].astype(jnp.float32),
        jnp.zeros((share, cols), jnp.float32),
    )
    full_ref[core, rows_of(me)] = reduced.astype(jnp.bfloat16)

    def gather(k, chip):
        return pltpu.make_async_remote_copy(
            src_ref=full_ref.at[core, rows_of(chip)],
            dst_ref=full_ref.at[core, rows_of(chip)],
            send_sem=send2_sem.at[k],
            recv_sem=recv2_sem.at[chip],
            device_id=device_of(lax.rem(me + k, chips)),
            device_id_type=MESH,
        )

    def forward(chip):
        return pltpu.make_async_remote_copy(
            src_ref=full_ref.at[core, rows_of(chip)],
            dst_ref=full_ref.at[core, rows_of(chip)],
            send_sem=last_send.at[chip],
            recv_sem=last_recv.at[chip],
            device_id=twin,
            device_id_type=MESH,
        )

    def forwarded(chip):
        return pltpu.make_async_remote_copy(
            src_ref=full_ref.at[other, rows_of(chip)],
            dst_ref=full_ref.at[other, rows_of(chip)],
            send_sem=last_send.at[chip],
            recv_sem=last_recv.at[chip],
            device_id=twin,
            device_id_type=MESH,
        )

    @pl.loop(1, chips)
    def _(k):
        gather(k, me).start()

    forward(me).start()

    @pl.loop(1, chips)
    def _(k):
        chip = lax.rem(me + k, chips)
        gather(k, chip).wait_recv()
        forward(chip).start()

    @pl.loop(0, chips)
    def _(chip):
        forwarded(chip).wait_recv()

    for h in range(2):
        side = slice(h * cols, (h + 1) * cols)
        for b in range(2):
            point_out[b, :, side] = full_ref[h, b * width : (b + 1) * width].astype(jnp.float32)
        head_out[h * head_rows : (h + 1) * head_rows, :] = full_ref[
            h, point_rows:small_row
        ].astype(jnp.float32)
        small_out[:, side] = full_ref[h, small_row : small_row + 16].astype(jnp.float32)[:8]

    pair.wait_send()

    @pl.loop(1, chips)
    def _(k):
        scatter(k).wait_send()
        gather(k, me).wait_send()

    @pl.loop(0, chips)
    def _(chip):
        forward(chip).wait_send()


def run_reduce(n_neg, n_rep, point, head, small):
    chips = n_neg * n_rep // 2
    width = point.shape[-1]
    cols = width // 2
    grain = 16 * chips
    used = 2 * width + head.shape[0] // 2 + 16
    total = -(-used // grain) * grain
    vmem = pl.BlockSpec(memory_space=pltpu.VMEM)
    dma = pltpu.SemaphoreType.DMA
    return pl.pallas_call(
        functools.partial(reduce_kernel, n_neg, n_rep),
        out_shape=[
            jax.ShapeDtypeStruct(point.shape, jnp.float32),
            jax.ShapeDtypeStruct(head.shape, jnp.float32),
            jax.ShapeDtypeStruct(small.shape, jnp.float32),
        ],
        in_specs=[vmem] * 3,
        out_specs=[vmem] * 3,
        scratch_shapes=[
            pltpu.VMEM((2, total, cols), jnp.bfloat16),
            pltpu.VMEM((total, cols), jnp.bfloat16),
            pltpu.VMEM((chips, total // chips, cols), jnp.bfloat16),
            pltpu.VMEM((2, total, cols), jnp.bfloat16),
            dma, dma,
            dma((chips,)), dma((chips,)), dma((chips,)), dma((chips,)),
            dma((chips,)), dma((chips,)),
        ],
        compiler_params=pltpu.CompilerParams(
            collective_id=1, has_side_effects=True, vmem_limit_bytes=VMEM_LIMIT
        ),
    )(point, head, small)


def local(
    n_neg,
    n_rep,
    goal_states,
    premise_states,
    goal_ids,
    premise_ids,
    positives,
    kernels,
    gains,
    weights,
    head_weight,
):
    goals, premises = goal_states[0], premise_states[0]
    goal_count, length, width = goals.shape
    total = goal_count + premises.shape[0]
    ids = jnp.concatenate([goal_ids[0], premise_ids[0]], axis=0)
    lens = jnp.sum((ids != 0).astype(jnp.int32), axis=1)
    *saved, pool_sums = run_forward(lens, goals, premises, kernels, gains, weights)

    def widen(rows, fill):
        gap = jnp.full((goal_count, rows.shape[1]), fill, rows.dtype)
        return jnp.concatenate([rows[:goal_count], gap, rows[goal_count:]], axis=0)

    pooled = widen(pool_sums[:, :SEQS].reshape(total, width), 0.0)
    spans = widen(lens.astype(jnp.float32)[:, None], 1.0)
    loss, pooled_grad, head_grad = run_contrast(
        n_neg, goal_count, pooled, spans, head_weight, positives.reshape(-1, 1)
    )
    upstream = jnp.concatenate([pooled_grad[:goal_count], pooled_grad[2 * goal_count :]], axis=0)
    point, small = run_backward(lens, saved, upstream[:, None, :], kernels, gains, weights)
    point, head, small = run_reduce(n_neg, n_rep, point, head_grad, small)
    return (
        loss[:, 0][None, :],
        small[:6].reshape(2, 3, width),
        small[6:],
        point,
        head,
    )


def solution(mesh):
    placed = (
        P("rep", "neg", None, None),
        P("rep", "neg", None, None),
        P("rep", "neg", None),
        P("rep", "neg", None),
        P("rep", None),
        P(),
        P(),
        P(),
        P(),
    )
    return jax.shard_map(
        functools.partial(local, mesh.shape["neg"], mesh.shape["rep"]),
        mesh=mesh,
        in_specs=placed,
        out_specs=(P("rep", "neg"), P(), P(), P(), P()),
        check_vma=False,
    )
```

time: 363 us -> 139 us (0.38)
  the two profiles are of different devices: /device:TPU:1 before, /device:TPU:31 now
where the time goes in v1:
time: 139 us; the launch traced here: 138 us
  Pallas kernels  120 us (86%)
  local copies, waits for them, and re-layouts  16.4 us (12%)
  other arithmetic  1.63 us (1%)
    pallas_call x1, Pallas kernels, run_reduce(): pl.pallas_call(functools.partial(reduce_kernel, n_neg, n_rep), out_shape=...  50.8 us
    pallas_call x1, Pallas kernels, run_forward(): pl.pallas_call(functools.partial(forward_kernel, goal_steps), grid_spec=p...  30.5 us
    pallas_call x1, Pallas kernels, run_backward(): pl.pallas_call(backward_kernel, grid_spec=pltpu.PrefetchScalarGridSpec(nu...  28.3 us
    pallas_call x1, Pallas kernels, run_contrast(): pl.pallas_call(functools.partial(contrast_kernel, n_neg, goal_count), out...  10.1 us
    unnamed x6, local copies, waits for them, and re-layouts  6.87 us

profile of v1, /device:TPU:31, one launch (start us, length us, event | category | flops | bytes accessed | tf_op | source)
XLA Modules:
  0.0 138.5 jit_solution(14891385053006089335)
XLA Ops:
  0.6 0.8 convert_reduce_fusion.lens_ref
  1.5 0.0 copy-start
  1.5 0.1 slice_bitcast_fusion
  1.6 0.1 pad.6.clone
  1.6 0.1 fusion
  1.7 1.3 copy.26.kern_ref
  3.0 0.7 copy.27.lens_ref
  3.7 1.4 copy.28.positive_ref
  5.1 30.5 %shard_map.128 = (bf16[40,128,512]{2,1,0:T(8,128)(2,1)}, bf16[40,128,512]{2,1,0:T(8,128)(2,1)}, bf16[40,128,512]{2,1,0:T(8,128)(2,1)}, bf16[40,128,512]{2,1,0:T(...) custom-call(s32[40]{0:T(128)} %copy-done, ...), custom_call_target="tpu_custom_call" | custom-call | tf_op jit(solution)/shard_map/pallas_call | solution.py:95
  35.6 0.8 slice.42
  36.4 0.9 slice.44
  37.4 0.7 pad_maximum_fusion.pooled_ref
  38.1 10.1 %shard_map.129 = (f32[8,128]{1,0:T(8,128)}, f32[48,512]{1,0:T(8,128)}, f32[512,256]{1,0:T(8,128)}) custom-call(f32[48,512]{1,0:T(8,128)} %pad_maximum_fusion.pooled_ref, f32[48,1]{1,0:T(8,128)} %copy.27.lens_ref, bf16[512,256]{1,0:T(8,128)(2,1)} %head_ref.1, s32[64,1]{1,0:T(8,128)} %copy.28.positive_ref), custom_call_target="tpu_custom_call" | custom-call | tf_op jit(solution)/shard_map/pallas_call | solution.py:224
  48.2 1.3 slice_reduce_fusion
  49.4 0.7 slice.51
  50.2 0.8 slice.52
  51.0 0.7 broadcast_in_dim.8.up_ref
  51.7 28.3 %shard_map.130 = (f32[2,512,512]{2,1,0:T(8,128)}, f32[8,512]{1,0:T(8,128)}) custom-call(s32[40]{0:T(128)} %copy-done, bf16[40,128,512]{2,1,0:T(8,128)(2,1)} %get-tuple-element.23.n0_ref, bf16[40,128,512]{2,1,0:T(8,128)(2,1)} %get-tuple-element.24.m0_ref, bf16[40,128,512]{2,1,0:T(8,128)(2,1)} %get-tuple-element.25.d0_ref, ...), custom_call_target="tpu_custom_call" | custom-call | tf_op jit(solution)/shard_map/pallas_call | solution.py:311
  80.0 50.8 %shard_map.131 = (f32[2,512,512]{2,1,0:T(8,128)}, f32[512,256]{1,0:T(8,128)}, f32[8,512]{1,0:T(8,128)}) custom-call(f32[2,512,512]{2,1,0:T(8,128)} %get-tuple-element.31.point_ref, f32[512,256]{1,0:T(8,128)} %get-tuple-element.32.head_ref, f32[8,512]{1,0:T(8,128)} %get-tuple-element.33.small_ref), custom_call_target="tpu_custom_call" | custom-call | tf_op jit(solution)/shard_map/pallas_call | solution.py:514
  130.9 1.3 slice.54
  132.2 0.7 reshape.22
  132.9 0.6 copy.30
  133.5 3.1 %copy.33 = f32[2,512,512]{2,1,0:T(8,128)} copy(f32[2,512,512]{2,1,0:T(8,128)} %get-tuple-element.60) | data formatting | bytes 4194304
  136.6 1.9 %copy.34 = f32[512,256]{1,0:T(8,128)} copy(f32[512,256]{1,0:T(8,128)} %get-tuple-element.61) | data formatting | bytes 1048576
  (8 shorter events, 0.1 us)
Async XLA Ops:
  1.5 3.6 %copy-start = (s32[40]{0:T(128)}, s32[40]{0:T(128)S(1)}, u32[]{:S(2)}) copy-start(s32[40]{0:T(128)S(1)} %convert_reduce_fusion.lens_ref) | copy-start | bytes 484

commit v2 on v1

v2 whole, which is shorter than its diff:
```python
import functools

import jax
import jax.numpy as jnp
from jax import lax
from jax.experimental import pallas as pl
from jax.experimental.pallas import tpu as pltpu
from jax.sharding import PartitionSpec as P

LOWER_DILATION = 4
UPPER_DILATION = 8
LOGIT_SCALE = 20.0
GELU_C = 0.7978845608028654
GELU_A = 0.044715
SEQS = 4
MESH = pl.DeviceIdType.MESH
VMEM_LIMIT = 56 * 1024 * 1024


def shift_down(values, dilation):
    zeros = jnp.zeros_like(values[:, :dilation])
    return jnp.concatenate([zeros, values[:, : values.shape[1] - dilation]], axis=1)


def shift_up(values, dilation):
    zeros = jnp.zeros_like(values[:, :dilation])
    return jnp.concatenate([values[:, dilation:], zeros], axis=1)


def gelu_and_slope(value):
    square = value * value
    half = 0.5 + 0.5 * jnp.tanh(value * (GELU_C + (GELU_C * GELU_A) * square))
    slope = half + value * (half - half * half) * (2.0 * GELU_C + (6.0 * GELU_C * GELU_A) * square)
    return value * half, slope


def length_mask(lens_ref, step, length):
    place = lax.broadcasted_iota(jnp.int32, (length, 1), 0)
    return jnp.stack(
        [(place < lens_ref[step * SEQS + s]).astype(jnp.float32) for s in range(SEQS)]
    )


def length_column(lens_ref, step):
    row = lax.broadcasted_iota(jnp.int32, (8, 1), 0)
    spans = jnp.ones((8, 1), jnp.float32)
    for s in range(SEQS):
        spans = jnp.where(row == s, lens_ref[step * SEQS + s].astype(jnp.float32), spans)
    return spans


def forward_kernel(
    goal_steps, lens_ref, goal_ref, prem_ref, kern_ref, gain_ref, weight_ref,
    n0_ref, m0_ref, d0_ref, n1_ref, m1_ref, d1_ref, inv_ref, pool_ref,
):
    step = pl.program_id(0)
    count, length, width = prem_ref.shape
    states = jnp.where(step < goal_steps, goal_ref[...], prem_ref[...])
    mask = length_mask(lens_ref, step, length)

    def block(hidden, b, dilation, n_ref, m_ref, d_ref):
        inverse = lax.rsqrt(jnp.mean(hidden * hidden, axis=-1, keepdims=True) + 1e-06) * mask
        unscaled = hidden * inverse
        n_ref[...] = unscaled.astype(jnp.bfloat16)
        taps = kern_ref[b] * gain_ref[b][None, :]
        mixed = (
            taps[0] * shift_down(unscaled, dilation)
            + taps[1] * unscaled
            + taps[2] * shift_up(unscaled, dilation)
        ).astype(jnp.bfloat16)
        m_ref[...] = mixed
        pre_act = jnp.dot(
            mixed.reshape(count * length, width), weight_ref[b], preferred_element_type=jnp.float32
        ).reshape(count, length, width)
        act, slope = gelu_and_slope(pre_act)
        d_ref[...] = slope.astype(jnp.bfloat16)
        return (hidden + act).astype(jnp.bfloat16), inverse

    first, _ = block(states.astype(jnp.float32), 0, LOWER_DILATION, n0_ref, m0_ref, d0_ref)
    second, inverse = block(first.astype(jnp.float32), 1, UPPER_DILATION, n1_ref, m1_ref, d1_ref)
    inv_ref[...] = jnp.broadcast_to(inverse, inv_ref.shape)
    row = lax.broadcasted_iota(jnp.int32, (8, count * length), 0)
    col = lax.broadcasted_iota(jnp.int32, (8, count * length), 1)
    picks = jnp.zeros((8, count * length), jnp.float32)
    for s in range(SEQS):
        own = (row == s) & (col >= s * length) & (col < s * length + lens_ref[step * SEQS + s])
        picks = jnp.where(own, 1.0, picks)
    sums = jnp.dot(
        picks.astype(jnp.bfloat16),
        second.reshape(count * length, width),
        preferred_element_type=jnp.float32,
    )
    pool_ref[...] = (sums / length_column(lens_ref, step))[None]


def run_forward(lens, goals, premises, kernels, gains, weights):
    goal_count, length, width = goals.shape
    goal_steps = goal_count // SEQS
    total = goal_count + premises.shape[0]
    steps = total // SEQS
    block = pl.BlockSpec((SEQS, length, width), lambda i, lens: (i, 0, 0))
    whole = lambda shape: pl.BlockSpec(shape, lambda i, lens: (0,) * len(shape))
    state = jax.ShapeDtypeStruct((total, length, width), jnp.bfloat16)
    return pl.pallas_call(
        functools.partial(forward_kernel, goal_steps),
        grid_spec=pltpu.PrefetchScalarGridSpec(
            num_scalar_prefetch=1,
            grid=(steps,),
            in_specs=[
                pl.BlockSpec(
                    (SEQS, length, width), lambda i, lens: (jnp.minimum(i, goal_steps - 1), 0, 0)
                ),
                pl.BlockSpec(
                    (SEQS, length, width), lambda i, lens: (jnp.maximum(i - goal_steps, 0), 0, 0)
                ),
                whole(kernels.shape),
                whole(gains.shape),
                whole(weights.shape),
            ],
            out_specs=[block] * 6
            + [
                pl.BlockSpec((SEQS, length, 128), lambda i, lens: (i, 0, 0)),
                pl.BlockSpec((1, 8, width), lambda i, lens: (i, 0, 0)),
            ],
        ),
        out_shape=[state] * 6
        + [
            jax.ShapeDtypeStruct((total, length, 128), jnp.float32),
            jax.ShapeDtypeStruct((steps, 8, width), jnp.float32),
        ],
        compiler_params=pltpu.CompilerParams(vmem_limit_bytes=VMEM_LIMIT),
    )(lens, goals, premises, kernels, gains, weights)


def contrast_kernel(
    n_neg, goal_count, pooled_ref, head_ref, positive_ref,
    loss_ref, pooled_grad_ref, head_grad_ref,
    units_ref, goal_all, prem_all, send_sem, recv_sem,
):
    me = lax.axis_index("neg")
    barrier = pltpu.get_barrier_semaphore()

    @pl.loop(1, n_neg)
    def _(k):
        pl.semaphore_signal(
            barrier, inc=1, device_id={"neg": lax.rem(me + k, n_neg)}, device_id_type=MESH
        )

    steps, _, width = pooled_ref.shape
    goal_steps = goal_count // SEQS
    prem_count = steps * SEQS - goal_count
    pieces = [pooled_ref[i, :SEQS] for i in range(steps)]
    gap = jnp.zeros((goal_count, width), jnp.float32)
    pooled = jnp.concatenate(pieces[:goal_steps] + [gap] + pieces[goal_steps:], axis=0).astype(
        jnp.bfloat16
    )
    head = head_ref[...]
    embedded = jnp.dot(pooled, head, preferred_element_type=jnp.float32)
    magnitude = jnp.sqrt(jnp.sum(embedded * embedded, axis=-1, keepdims=True) + 1e-06)
    unit = embedded / magnitude
    units_ref[me] = unit.astype(jnp.bfloat16)
    pl.semaphore_wait(barrier, n_neg - 1)

    def copy_to(k):
        peer = lax.rem(me + k, n_neg)
        return pltpu.make_async_remote_copy(
            src_ref=units_ref.at[me],
            dst_ref=units_ref.at[me],
            send_sem=send_sem.at[k],
            recv_sem=recv_sem.at[me],
            device_id={"neg": peer},
            device_id_type=MESH,
        )

    @pl.loop(1, n_neg)
    def _(k):
        copy_to(k).start()

    @pl.loop(1, n_neg)
    def _(k):
        source = lax.rem(me + k, n_neg)
        pltpu.make_async_remote_copy(
            src_ref=units_ref.at[source],
            dst_ref=units_ref.at[source],
            send_sem=send_sem.at[k],
            recv_sem=recv_sem.at[source],
            device_id={"neg": source},
            device_id_type=MESH,
        ).wait_recv()

    everyone = units_ref[...].astype(jnp.float32)
    embed = everyone.shape[-1]
    goals = everyone[:, :goal_count].reshape(n_neg * goal_count, embed).astype(jnp.bfloat16)
    premises = everyone[:, 2 * goal_count :].reshape(n_neg * prem_count, embed).astype(jnp.bfloat16)
    scores = LOGIT_SCALE * lax.dot_general(
        premises, goals, (((1,), (1,)), ((), ())), preferred_element_type=jnp.float32
    )
    expon = jnp.exp(scores)
    total = jnp.sum(expon, axis=0, keepdims=True)
    places = lax.broadcasted_iota(jnp.int32, scores.shape, 0)
    onehot = (places == positive_ref[...]).astype(jnp.float32)
    loss = jnp.log(total) - jnp.sum(scores * onehot, axis=0, keepdims=True)
    group = (n_neg * goal_count, goal_count)
    pick = (
        lax.broadcasted_iota(jnp.int32, group, 0)
        == me * goal_count + lax.broadcasted_iota(jnp.int32, group, 1)
    ).astype(jnp.float32)
    loss_ref[...] = jnp.dot(
        jnp.broadcast_to(loss, (8, loss.shape[1])),
        pick,
        precision=lax.Precision.HIGHEST,
        preferred_element_type=jnp.float32,
    )[:1]
    score_grad = ((expon / total - onehot) / goal_count).astype(jnp.bfloat16)
    goal_all[...] = LOGIT_SCALE * lax.dot_general(
        score_grad, premises, (((0,), (0,)), ((), ())), preferred_element_type=jnp.float32
    )
    prem_all[...] = LOGIT_SCALE * jnp.dot(score_grad, goals, preferred_element_type=jnp.float32)
    own_goals = pl.ds(pl.multiple_of(me * goal_count, goal_count), goal_count)
    own_prems = pl.ds(pl.multiple_of(me * prem_count, prem_count), prem_count)
    own_goal_grad = goal_all[own_goals, :]
    unit_grad = jnp.concatenate(
        [own_goal_grad, jnp.zeros_like(own_goal_grad), prem_all[own_prems, :]], axis=0
    )
    embed_grad = (
        (unit_grad - unit * jnp.sum(unit * unit_grad, axis=-1, keepdims=True)) / magnitude
    ).astype(jnp.bfloat16)
    head_grad = lax.dot_general(
        pooled, embed_grad, (((0,), (0,)), ((), ())), preferred_element_type=jnp.float32
    )
    head_grad_ref[...] = head_grad.astype(jnp.bfloat16).reshape(head_grad_ref.shape)
    pooled_grad = lax.dot_general(
        embed_grad, head, (((1,), (1,)), ((), ())), preferred_element_type=jnp.float32
    )
    for i in range(steps):
        start = i * SEQS + (goal_count if i >= goal_steps else 0)
        pooled_grad_ref[i, :SEQS] = pooled_grad[start : start + SEQS]
        pooled_grad_ref[i, SEQS:] = jnp.zeros((8 - SEQS, width), jnp.float32)

    @pl.loop(1, n_neg)
    def _(k):
        copy_to(k).wait_send()


def run_contrast(n_neg, goal_count, pooled, head, positives):
    steps, _, width = pooled.shape
    embed = head.shape[1]
    prem_count = steps * SEQS - goal_count
    vmem = pl.BlockSpec(memory_space=pltpu.VMEM)
    return pl.pallas_call(
        functools.partial(contrast_kernel, n_neg, goal_count),
        out_shape=[
            jax.ShapeDtypeStruct((1, goal_count), jnp.float32),
            jax.ShapeDtypeStruct(pooled.shape, jnp.float32),
            jax.ShapeDtypeStruct((2, width // 2, embed), jnp.bfloat16),
        ],
        in_specs=[vmem] * 3,
        out_specs=[vmem] * 3,
        scratch_shapes=[
            pltpu.VMEM((n_neg, 2 * goal_count + prem_count, embed), jnp.bfloat16),
            pltpu.VMEM((n_neg * goal_count, embed), jnp.float32),
            pltpu.VMEM((n_neg * prem_count, embed), jnp.float32),
            pltpu.SemaphoreType.DMA((n_neg,)),
            pltpu.SemaphoreType.DMA((n_neg,)),
        ],
        compiler_params=pltpu.CompilerParams(
            collective_id=0, has_side_effects=True, vmem_limit_bytes=VMEM_LIMIT
        ),
    )(pooled, head, positives)


def upper_kernel(lens_ref, m_ref, d_ref, up_ref, act_ref, scaled_ref, point_ref, sum_ref):
    step = pl.program_id(0)
    count, length, width = m_ref.shape
    tokens = count * length

    @pl.when(step == 0)
    def _():
        sum_ref[...] = jnp.zeros_like(sum_ref)

    rows = up_ref[0] / length_column(lens_ref, step)
    scaled_ref[...] = rows[None]
    mask = length_mask(lens_ref, step, length)
    upstream = jnp.stack([rows[s : s + 1] for s in range(SEQS)]) * mask
    act_grad = (upstream * d_ref[...].astype(jnp.float32)).astype(jnp.bfloat16)
    act_ref[...] = act_grad
    sum_ref[...] += lax.dot_general(
        m_ref[...].reshape(tokens, width),
        act_grad.reshape(tokens, width),
        (((0,), (0,)), ((), ())),
        preferred_element_type=jnp.float32,
    )

    @pl.when(step == pl.num_programs(0) - 1)
    def _():
        for h in range(2):
            point_ref[h] = sum_ref[:, h * width // 2 : (h + 1) * width // 2].astype(jnp.bfloat16)


def run_upper(lens, mixed, slope, pooled_grad):
    total, length, width = mixed.shape
    steps = total // SEQS
    block = pl.BlockSpec((SEQS, length, width), lambda i, lens: (i, 0, 0))
    rows = pl.BlockSpec((1, 8, width), lambda i, lens: (i, 0, 0))
    return pl.pallas_call(
        upper_kernel,
        grid_spec=pltpu.PrefetchScalarGridSpec(
            num_scalar_prefetch=1,
            grid=(steps,),
            in_specs=[block, block, rows],
            out_specs=[
                block,
                rows,
                pl.BlockSpec((2, width, width // 2), lambda i, lens: (0, 0, 0)),
            ],
            scratch_shapes=[pltpu.VMEM((width, width), jnp.float32)],
        ),
        out_shape=[
            jax.ShapeDtypeStruct(mixed.shape, jnp.bfloat16),
            jax.ShapeDtypeStruct(pooled_grad.shape, jnp.float32),
            jax.ShapeDtypeStruct((2, width, width // 2), jnp.bfloat16),
        ],
        compiler_params=pltpu.CompilerParams(vmem_limit_bytes=VMEM_LIMIT),
    )(lens, mixed, slope, pooled_grad)


class Exchange:
    def __init__(self, n_neg, n_rep, mine, pair, slots, full, sems):
        self.mine, self.pair, self.slots, self.full = mine, pair, slots, full
        (self.pair_sems, self.scatter_send, self.scatter_recv,
         self.gather_send, self.gather_recv, self.last_send, self.last_recv) = sems
        self.half_rep = n_rep // 2
        self.chips = n_neg * self.half_rep
        neg, rep = lax.axis_index("neg"), lax.axis_index("rep")
        self.core = lax.rem(rep, 2)
        self.other = 1 - self.core
        self.me = neg * self.half_rep + rep // 2
        self.twin = {"neg": neg, "rep": rep + 1 - 2 * self.core}
        self.share = mine.shape[1] // self.chips

    def device_of(self, chip):
        return {
            "neg": chip // self.half_rep,
            "rep": 2 * lax.rem(chip, self.half_rep) + self.core,
        }

    def peer(self, k):
        return lax.rem(self.me + k, self.chips)

    def rows_of(self, chip):
        return pl.ds(pl.multiple_of(chip * self.share, 16), self.share)

    def copy(self, src, dst, send, recv, device):
        return pltpu.make_async_remote_copy(
            src_ref=src, dst_ref=dst, send_sem=send, recv_sem=recv,
            device_id=device, device_id_type=MESH,
        )

    def pair_copy(self):
        return self.copy(
            self.mine.at[self.other], self.pair, self.pair_sems.at[0], self.pair_sems.at[1],
            self.twin,
        )

    def pair_sum(self):
        self.pair_copy().wait_recv()
        self.mine[self.core] = (
            self.mine[self.core].astype(jnp.float32) + self.pair[...].astype(jnp.float32)
        ).astype(jnp.bfloat16)

    def scatter(self, k):
        chip = self.peer(k)
        return self.copy(
            self.mine.at[self.core, self.rows_of(chip)], self.slots.at[self.me],
            self.scatter_send.at[k], self.scatter_recv.at[self.me], self.device_of(chip),
        )

    def start_scatter(self):
        @pl.loop(1, self.chips)
        def _(k):
            self.scatter(k).start()

        self.slots[self.me] = self.mine[self.core, self.rows_of(self.me)]

    def finish_scatter(self):
        @pl.loop(1, self.chips)
        def _(k):
            chip = self.peer(k)
            self.copy(
                self.slots.at[chip], self.slots.at[chip],
                self.scatter_send.at[k], self.scatter_recv.at[chip], self.device_of(chip),
            ).wait_recv()

        reduced = lax.fori_loop(
            0,
            self.chips,
            lambda c, acc: acc + self.slots[c].astype(jnp.float32),
            jnp.zeros(self.slots.shape[1:], jnp.float32),
        )
        self.full[self.core, self.rows_of(self.me)] = reduced.astype(jnp.bfloat16)

    def gather(self, k, chip):
        block = self.full.at[self.core, self.rows_of(chip)]
        return self.copy(
            block, block, self.gather_send.at[k], self.gather_recv.at[chip],
            self.device_of(self.peer(k)),
        )

    def forward(self, side, chip):
        block = self.full.at[side, self.rows_of(chip)]
        return self.copy(
            block, block, self.last_send.at[chip], self.last_recv.at[chip], self.twin
        )

    def start_gather(self):
        @pl.loop(1, self.chips)
        def _(k):
            self.gather(k, self.me).start()

        self.forward(self.core, self.me).start()

    def finish_gather(self):
        @pl.loop(1, self.chips)
        def _(k):
            chip = self.peer(k)
            self.gather(k, chip).wait_recv()
            self.forward(self.core, chip).start()

    def finish_last(self):
        @pl.loop(0, self.chips)
        def _(chip):
            self.forward(self.other, chip).wait_recv()

    def finish_sends(self):
        self.pair_copy().wait_send()

        @pl.loop(1, self.chips)
        def _(k):
            self.scatter(k).wait_send()
            self.gather(k, self.me).wait_send()

        @pl.loop(0, self.chips)
        def _(chip):
            self.forward(self.core, chip).wait_send()


def lower_kernel(
    n_neg, n_rep, steps,
    n0_ref, m0_ref, d0_ref, n1_ref, a1_ref, inv_ref, up_ref,
    kern_ref, gain_ref, weight_ref, point1_ref, head_ref,
    point_out, head_out, depth_out, gain_out,
    sum_ref, sums_ref,
    mine1, pair1, slots1, full1, mine0, pair0, slots0, full0,
    small_mine, small_pair, small_slots, small_full,
    ps1, ss1, sr1, gs1, gr1, ls1, lr1,
    ps0, ss0, sr0, gs0, gr0, ls0, lr0,
    small_pair_sems, small_send, small_recv, small_last,
):
    step = pl.program_id(0)
    count, length, width = n0_ref.shape
    tokens = count * length
    cols = width // 2
    head_rows = head_ref.shape[1]
    upper = Exchange(n_neg, n_rep, mine1, pair1, slots1, full1, (ps1, ss1, sr1, gs1, gr1, ls1, lr1))
    lower = Exchange(n_neg, n_rep, mine0, pair0, slots0, full0, (ps0, ss0, sr0, gs0, gr0, ls0, lr0))
    chips, core, other, me, twin = lower.chips, lower.core, lower.other, lower.me, lower.twin

    @pl.when(step == 0)
    def _():
        barrier = pltpu.get_barrier_semaphore()
        pl.semaphore_signal(barrier, inc=1, device_id=twin, device_id_type=MESH)

        @pl.loop(1, chips)
        def _(k):
            pl.semaphore_signal(
                barrier, inc=1, device_id=lower.device_of(lower.peer(k)), device_id_type=MESH
            )

        sum_ref[...] = jnp.zeros_like(sum_ref)
        sums_ref[...] = jnp.zeros_like(sums_ref)
        for h in range(2):
            mine1[h, :width] = point1_ref[h]
            mine1[h, width : width + head_rows] = head_ref[h]
            spare = mine1.shape[1] - width - head_rows
            if spare:
                mine1[h, width + head_rows :] = jnp.zeros((spare, cols), jnp.bfloat16)
        pl.semaphore_wait(barrier, chips)
        upper.pair_copy().start()

    @pl.when(step == min(1, steps - 1))
    def _():
        upper.pair_sum()
        upper.start_scatter()

    @pl.when(step == steps // 2)
    def _():
        upper.finish_scatter()
        upper.start_gather()

    def fold(values):
        return jnp.sum(values.reshape(tokens // 8, 8, width), axis=0)

    def conv_terms(act_grad, b, dilation, unscaled):
        conv = lax.dot_general(
            act_grad.reshape(tokens, width),
            weight_ref[b],
            (((1,), (1,)), ((), ())),
            preferred_element_type=jnp.float32,
        ).reshape(count, length, width)
        above = shift_up(conv, dilation)
        below = shift_down(conv, dilation)
        sums_ref[b, 0] += fold(above * unscaled)
        sums_ref[b, 1] += fold(conv * unscaled)
        sums_ref[b, 2] += fold(below * unscaled)
        return above, conv, below

    unscaled = n1_ref[...].astype(jnp.float32)
    above, conv, below = conv_terms(a1_ref[...], 1, UPPER_DILATION, unscaled)
    taps = kern_ref[1] * gain_ref[1][None, :]
    scaled = taps[0] * above + taps[1] * conv + taps[2] * below
    mean = jnp.mean(scaled * unscaled, axis=-1, keepdims=True)
    inverse = inv_ref[:, :, :1]
    rows = up_ref[0]
    upstream = jnp.stack([rows[s : s + 1] for s in range(SEQS)])
    incoming = jnp.where(inverse > 0.0, upstream, 0.0) + inverse * (scaled - unscaled * mean)
    act_grad = (incoming * d0_ref[...].astype(jnp.float32)).astype(jnp.bfloat16)
    sum_ref[...] += lax.dot_general(
        m0_ref[...].reshape(tokens, width),
        act_grad.reshape(tokens, width),
        (((0,), (0,)), ((), ())),
        preferred_element_type=jnp.float32,
    )
    conv_terms(act_grad, 0, LOWER_DILATION, n0_ref[...].astype(jnp.float32))

    @pl.when(step == steps - 1)
    def _():
        spare = mine0.shape[1] - width
        for h in range(2):
            mine0[h, :width] = sum_ref[:, h * cols : (h + 1) * cols].astype(jnp.bfloat16)
            if spare:
                mine0[h, width:] = jnp.zeros((spare, cols), jnp.bfloat16)
        lower.pair_copy().start()
        rows = []
        for b in range(2):
            plain = jnp.sum(sums_ref[b], axis=1)
            rows.append(plain * gain_ref[b][None, :])
            rows.append(jnp.sum(plain * kern_ref[b], axis=0, keepdims=True))
        small = jnp.concatenate([rows[0], rows[2], rows[1], rows[3]], axis=0)
        for h in range(2):
            small_mine[h] = small[:, h * cols : (h + 1) * cols]
        small_copy = lower.copy(
            small_mine.at[other], small_pair, small_pair_sems.at[0], small_pair_sems.at[1], twin
        )
        small_copy.start()
        lower.pair_sum()
        lower.start_scatter()
        small_copy.wait_recv()
        small_slots[me] = small_mine[core] + small_pair[...]

        def small_send_to(k):
            return lower.copy(
                small_slots.at[me], small_slots.at[me], small_send.at[k], small_recv.at[me],
                lower.device_of(lower.peer(k)),
            )

        @pl.loop(1, chips)
        def _(k):
            small_send_to(k).start()

        upper.finish_gather()
        lower.finish_scatter()
        lower.start_gather()

        @pl.loop(1, chips)
        def _(k):
            chip = lower.peer(k)
            lower.copy(
                small_slots.at[chip], small_slots.at[chip], small_send.at[k],
                small_recv.at[chip], lower.device_of(chip),
            ).wait_recv()

        small_full[core] = lax.fori_loop(
            0, chips, lambda c, acc: acc + small_slots[c], jnp.zeros((8, cols), jnp.float32)
        )

        def small_forward(side):
            return lower.copy(
                small_full.at[side], small_full.at[side], small_last.at[0], small_last.at[1], twin
            )

        small_forward(core).start()
        upper.finish_last()
        for h in range(2):
            side = slice(h * cols, (h + 1) * cols)
            point_out[1, :, side] = full1[h, :width]
            head_out[h] = full1[h, width : width + head_rows]
        lower.finish_gather()
        small_forward(other).wait_recv()
        for h in range(2):
            side = slice(h * cols, (h + 1) * cols)
            depth_out[0, :, side] = small_full[h, 0:3]
            depth_out[1, :, side] = small_full[h, 3:6]
            gain_out[:, side] = small_full[h, 6:8]
        lower.finish_last()
        for h in range(2):
            point_out[0, :, h * cols : (h + 1) * cols] = full0[h, :width]
        upper.finish_sends()
        lower.finish_sends()
        small_copy.wait_send()
        small_forward(core).wait_send()

        @pl.loop(1, chips)
        def _(k):
            small_send_to(k).wait_send()


def run_lower(n_neg, n_rep, saved, pooled_grad, kernels, gains, weights, point1, head):
    total, length, width = saved[0].shape
    steps = total // SEQS
    chips = n_neg * n_rep // 2
    cols = width // 2
    grain = 16 * chips
    rows1 = -(-(width + head.shape[1]) // grain) * grain
    rows0 = -(-width // grain) * grain
    block = pl.BlockSpec((SEQS, length, width), lambda i: (i, 0, 0))
    whole = lambda shape: pl.BlockSpec(shape, lambda i: (0,) * len(shape))
    dma = pltpu.SemaphoreType.DMA

    def buffers(rows):
        return [
            pltpu.VMEM((2, rows, cols), jnp.bfloat16),
            pltpu.VMEM((rows, cols), jnp.bfloat16),
            pltpu.VMEM((chips, rows // chips, cols), jnp.bfloat16),
            pltpu.VMEM((2, rows, cols), jnp.bfloat16),
        ]

    outs = [
        jax.ShapeDtypeStruct(weights.shape, jnp.bfloat16),
        jax.ShapeDtypeStruct(head.shape, jnp.bfloat16),
        jax.ShapeDtypeStruct(kernels.shape, jnp.float32),
        jax.ShapeDtypeStruct(gains.shape, jnp.float32),
    ]
    return pl.pallas_call(
        functools.partial(lower_kernel, n_neg, n_rep, steps),
        grid=(steps,),
        in_specs=[block] * 5
        + [
            pl.BlockSpec((SEQS, length, 128), lambda i: (i, 0, 0)),
            pl.BlockSpec((1, 8, width), lambda i: (i, 0, 0)),
            whole(kernels.shape),
            whole(gains.shape),
            whole(weights.shape),
            whole(point1.shape),
            whole(head.shape),
        ],
        out_specs=[whole(out.shape) for out in outs],
        out_shape=outs,
        scratch_shapes=[
            pltpu.VMEM((width, width), jnp.float32),
            pltpu.VMEM((2, 3, 8, width), jnp.float32),
            *buffers(rows1),
            *buffers(rows0),
            pltpu.VMEM((2, 8, cols), jnp.float32),
            pltpu.VMEM((8, cols), jnp.float32),
            pltpu.VMEM((chips, 8, cols), jnp.float32),
            pltpu.VMEM((2, 8, cols), jnp.float32),
            *([dma((2,))] + [dma((chips,))] * 6),
            *([dma((2,))] + [dma((chips,))] * 6),
            dma((2,)),
            dma((chips,)),
            dma((chips,)),
            dma((2,)),
        ],
        compiler_params=pltpu.CompilerParams(
            collective_id=1, has_side_effects=True, vmem_limit_bytes=VMEM_LIMIT
        ),
    )(*saved, pooled_grad, kernels, gains, weights, point1, head)


def local(
    n_neg,
    n_rep,
    goal_states,
    premise_states,
    goal_ids,
    premise_ids,
    positives,
    kernels,
    gains,
    weights,
    head_weight,
):
    goals, premises = goal_states[0], premise_states[0]
    goal_count, length, width = goals.shape
    total = goal_count + premises.shape[0]
    ids = jnp.concatenate([goal_ids[0], premise_ids[0]], axis=0)
    lens = jnp.sum((ids != 0).astype(jnp.int32), axis=1)
    n0, m0, d0, n1, m1, d1, inverse, pooled = run_forward(
        lens, goals, premises, kernels, gains, weights
    )
    loss, pooled_grad, head = run_contrast(n_neg, goal_count, pooled, head_weight, positives)
    act1, upstream, point1 = run_upper(lens, m1, d1, pooled_grad)
    point, head, depth, gain = run_lower(
        n_neg, n_rep, (n0, m0, d0, n1, act1, inverse), upstream, kernels, gains, weights,
        point1, head,
    )
    return (
        loss,
        depth,
        gain,
        point.astype(jnp.float32),
        head.reshape(head_weight.shape).astype(jnp.float32),
    )


def solution(mesh):
    placed = (
        P("rep", "neg", None, None),
        P("rep", "neg", None, None),
        P("rep", "neg", None),
        P("rep", "neg", None),
        P("rep", None),
        P(),
        P(),
        P(),
        P(),
    )
    return jax.shard_map(
        functools.partial(local, mesh.shape["neg"], mesh.shape["rep"]),
        mesh=mesh,
        in_specs=placed,
        out_specs=(P("rep", "neg"), P(), P(), P(), P()),
        check_vma=False,
    )
```

time: 139 us -> 120 us (0.86)
  the two profiles are of different devices: /device:TPU:31 before, /device:TPU:1 now
where the time goes in v2:
time: 120 us; the launch traced here: 119 us
  Pallas kernels  108 us (90%)
  other arithmetic  5.96 us (5%)
  local copies, waits for them, and re-layouts  4.41 us (4%)
    pallas_call x1, Pallas kernels, run_lower(): pl.pallas_call(functools.partial(lower_kernel, n_neg, n_rep, steps), grid...  53.5 us
    pallas_call x1, Pallas kernels, run_forward(): pl.pallas_call(functools.partial(forward_kernel, goal_steps), grid_spec=p...  30.6 us
    pallas_call x1, Pallas kernels, run_upper(): pl.pallas_call(upper_kernel, grid_spec=pltpu.PrefetchScalarGridSpec(num_s...  12.5 us
    pallas_call x1, Pallas kernels, run_contrast(): pl.pallas_call(functools.partial(contrast_kernel, n_neg, goal_count), out...  11.2 us
    unnamed x6, local copies, waits for them, and re-layouts  4.41 us
    convert_element_type x1, other arithmetic, local(): point.astype(jnp.float32)  2.83 us

profile of v2, /device:TPU:1, one launch (start us, length us, event | category | flops | bytes accessed | tf_op | source)
XLA Modules:
  0.0 118.9 jit_solution(6405275874562190114)
XLA Ops:
  0.6 1.3 %convert_reduce_fusion.lens_ref = s32[40]{0:T(128)} fusion(s32[32,128]{1,0:T(8,128)} %bitcast.9, s32[8,128]{1,0:T(8,128)} %bitcast.10), kind=kLoop, calls=%fused_computation.2 | loop fusion | flops 20440 | bytes 20640 | tf_op jit(solution)/shard_map/reduce_sum | solution.py:697
  2.0 1.3 %copy.14.kern_ref = f32[2,3,512]{2,1,0:T(4,128)} copy(f32[2,3,512]{2,0,1:T(2,128)} %param.14) | data formatting | bytes 24576 | tf_op args[5]
  3.3 30.6 %shard_map.128 = (bf16[40,128,512]{2,1,0:T(8,128)(2,1)}, bf16[40,128,512]{2,1,0:T(8,128)(2,1)}, bf16[40,128,512]{2,1,0:T(8,128)(2,1)}, bf16[40,128,512]{2,1,0:T(...) custom-call(s32[40]{0:T(128)} %convert_reduce_fusion.lens_ref, ...), custom_call_target="tpu_custom_call" | custom-call | tf_op jit(solution)/shard_map/pallas_call | solution.py:104
  33.9 11.2 %shard_map.129 = (f32[1,8]{1,0:T(1,128)}, f32[10,8,512]{2,1,0:T(8,128)}, bf16[2,256,256]{2,1,0:T(8,128)(2,1)}) custom-call(f32[10,8,512]{2,1,0:T(8,128)} %get-tuple-element.23.pooled_ref, bf16[512,256]{1,0:T(8,128)(2,1)} %head_ref.1, s32[1,64]{1,0:T(1,128)} %positive_ref.1), custom_call_target="tpu_custom_call" | custom-call | tf_op jit(solution)/shard_map/pallas_call | solution.py:250
  45.1 12.5 %shard_map.130 = (bf16[40,128,512]{2,1,0:T(8,128)(2,1)}, f32[10,8,512]{2,1,0:T(8,128)}, bf16[2,512,256]{2,1,0:T(8,128)(2,1)}) custom-call(s32[40]{0:T(128)} %convert_reduce_fusion.lens_ref, bf16[40,128,512]{2,1,0:T(8,128)(2,1)} %get-tuple-element.29.m_ref, bf16[40,128,512]{2,1,0:T(8,128)(2,1)} %get-tuple-element.30.d_ref, f32[10,8,512]{2,1,0:T(8,128)} %get-tuple-element.31.up_ref), custom_call_target="tpu_custom_call" | custom-call | tf_op jit(solution)/shard_map/pallas_call | solution.py:305
  57.6 0.0 copy-start
  57.6 53.5 %shard_map.131 = (bf16[2,512,512]{2,1,0:T(8,128)(2,1)}, bf16[2,256,256]{2,1,0:T(8,128)(2,1)}, f32[2,3,512]{2,1,0:T(4,128)}, f32[2,512]{1,0:T(2,128)}) custom-call(bf16[40,128,512]{2,1,0:T(8,128)(2,1)} %get-tuple-element.25.n0_ref, bf16[40,128,512]{2,1,0:T(8,128)(2,1)} %get-tuple-element.26.m0_ref, bf16[40,128,512]{2,1,0:T(8,128)(2,1)} %get-tuple-element.27.d0_ref, ...), custom_call_target="tpu_custom_call" | custom-call | tf_op jit(solution)/shard_map/pallas_call | solution.py:643
  111.2 1.3 %copy.16 = f32[2,3,512]{2,0,1:T(2,128)} copy(f32[2,3,512]{2,1,0:T(4,128)} %get-tuple-element.42) | data formatting | bytes 24576
  112.5 1.8 %bitcast_convert_fusion = f32[512,256]{1,0:T(8,128)} fusion(bf16[2,256,256]{2,1,0:T(8,128)(2,1)} %get-tuple-element.40), kind=kLoop, calls=%fused_computation | loop fusion | flops 131072 | bytes 786432 | tf_op jit(solution)/shard_map/convert_element_type | solution.py:712
  114.3 2.8 %convert_element_type.13 = f32[2,512,512]{2,1,0:T(8,128)} convert(bf16[2,512,512]{2,1,0:T(8,128)(2,1)} %get-tuple-element.39) | non-fusion elementwise | flops 524288 | bytes 3145728 | tf_op jit(solution)/shard_map/convert_element_type | solution.py:711
  117.1 0.0 copy-done
  117.1 0.5 copy.19
  117.6 1.3 %copy.20 = f32[2,512]{1,0:T(2,128)} copy(f32[2,512]{1,0:T(2,128)} %get-tuple-element.53) | data formatting | bytes 8192
Async XLA Ops:
  57.6 59.5 %copy-start = (f32[1,8]{1,0:T(1,128)S(1)}, f32[1,8]{1,0:T(1,128)}, u32[]{:S(2)}) copy-start(f32[1,8]{1,0:T(1,128)} %get-tuple-element.51) | copy-start | bytes 100

commit v3 on v2

--- a/solution.py
+++ b/solution.py
@@ -29,8 +29,10 @@
 
 def gelu_and_slope(value):
     square = value * value
-    half = 0.5 + 0.5 * jnp.tanh(value * (GELU_C + (GELU_C * GELU_A) * square))
-    slope = half + value * (half - half * half) * (2.0 * GELU_C + (6.0 * GELU_C * GELU_A) * square)
+    bend = jnp.tanh(value * (GELU_C + (GELU_C * GELU_A) * square))
+    half = 0.5 + 0.5 * bend
+    rest = 0.5 - 0.5 * bend
+    slope = half + (half * rest) * (value * (2.0 * GELU_C + (6.0 * GELU_C * GELU_A) * square))
     return value * half, slope
 
 
@@ -58,7 +60,8 @@
     states = jnp.where(step < goal_steps, goal_ref[...], prem_ref[...])
     mask = length_mask(lens_ref, step, length)
 
-    def block(hidden, b, dilation, n_ref, m_ref, d_ref):
+    def block(narrow, b, dilation, n_ref, m_ref, d_ref):
+        hidden = narrow.astype(jnp.float32)
         inverse = lax.rsqrt(jnp.mean(hidden * hidden, axis=-1, keepdims=True) + 1e-06) * mask
         unscaled = hidden * inverse
         n_ref[...] = unscaled.astype(jnp.bfloat16)
@@ -72,12 +75,12 @@
         pre_act = jnp.dot(
             mixed.reshape(count * length, width), weight_ref[b], preferred_element_type=jnp.float32
         ).reshape(count, length, width)
-        act, slope = gelu_and_slope(pre_act)
-        d_ref[...] = slope.astype(jnp.bfloat16)
-        return (hidden + act).astype(jnp.bfloat16), inverse
-
-    first, _ = block(states.astype(jnp.float32), 0, LOWER_DILATION, n0_ref, m0_ref, d0_ref)
-    second, inverse = block(first.astype(jnp.float32), 1, UPPER_DILATION, n1_ref, m1_ref, d1_ref)
+        act, slope = gelu_and_slope(pre_act.astype(jnp.bfloat16))
+        d_ref[...] = slope
+        return narrow + act, inverse
+
+    first, _ = block(states, 0, LOWER_DILATION, n0_ref, m0_ref, d0_ref)
+    second, inverse = block(first, 1, UPPER_DILATION, n1_ref, m1_ref, d1_ref)
     inv_ref[...] = jnp.broadcast_to(inverse, inv_ref.shape)
     row = lax.broadcasted_iota(jnp.int32, (8, count * length), 0)
     col = lax.broadcasted_iota(jnp.int32, (8, count * length), 1)
@@ -281,8 +284,8 @@
     rows = up_ref[0] / length_column(lens_ref, step)
     scaled_ref[...] = rows[None]
     mask = length_mask(lens_ref, step, length)
-    upstream = jnp.stack([rows[s : s + 1] for s in range(SEQS)]) * mask
-    act_grad = (upstream * d_ref[...].astype(jnp.float32)).astype(jnp.bfloat16)
+    upstream = (jnp.stack([rows[s : s + 1] for s in range(SEQS)]) * mask).astype(jnp.bfloat16)
+    act_grad = upstream * d_ref[...]
     act_ref[...] = act_grad
     sum_ref[...] += lax.dot_general(
         m_ref[...].reshape(tokens, width),
@@ -484,15 +487,18 @@
             spare = mine1.shape[1] - width - head_rows
             if spare:
                 mine1[h, width + head_rows :] = jnp.zeros((spare, cols), jnp.bfloat16)
-        pl.semaphore_wait(barrier, chips)
+
+    @pl.when(step == 1)
+    def _():
+        pl.semaphore_wait(pltpu.get_barrier_semaphore(), chips)
         upper.pair_copy().start()
 
-    @pl.when(step == min(1, steps - 1))
+    @pl.when(step == 2)
     def _():
         upper.pair_sum()
         upper.start_scatter()
 
-    @pl.when(step == steps // 2)
+    @pl.when(step == (2 * steps) // 3)
     def _():
         upper.finish_scatter()
         upper.start_gather()
@@ -523,7 +529,7 @@
     rows = up_ref[0]
     upstream = jnp.stack([rows[s : s + 1] for s in range(SEQS)])
     incoming = jnp.where(inverse > 0.0, upstream, 0.0) + inverse * (scaled - unscaled * mean)
-    act_grad = (incoming * d0_ref[...].astype(jnp.float32)).astype(jnp.bfloat16)
+    act_grad = incoming.astype(jnp.bfloat16) * d0_ref[...]
     sum_ref[...] += lax.dot_general(
         m0_ref[...].reshape(tokens, width),
         act_grad.reshape(tokens, width),
@@ -617,6 +623,7 @@
 def run_lower(n_neg, n_rep, saved, pooled_grad, kernels, gains, weights, point1, head):
     total, length, width = saved[0].shape
     steps = total // SEQS
+    assert steps >= 5
     chips = n_neg * n_rep // 2
     cols = width // 2
     grain = 16 * chips
@@ -675,6 +682,37 @@
             collective_id=1, has_side_effects=True, vmem_limit_bytes=VMEM_LIMIT
         ),
     )(*saved, pooled_grad, kernels, gains, weights, point1, head)
+
+
+def widen_kernel(point_ref, head_ref, loss_ref, point_out, head_out, loss_out):
+    point_out[...] = point_ref[...].astype(jnp.float32)
+    head_out[...] = head_ref[0].astype(jnp.float32)
+    loss_out[...] = loss_ref[...]
+
+
+def run_widen(point, head, loss):
+    _, width, embed = head.shape
+    part = point.shape[1] // 2
+    rows = width // 2
+    return pl.pallas_call(
+        widen_kernel,
+        grid=(4,),
+        in_specs=[
+            pl.BlockSpec((1, part, point.shape[2]), lambda i: (i // 2, i % 2, 0)),
+            pl.BlockSpec((1, rows, embed), lambda i: (i // 2, i % 2, 0)),
+            pl.BlockSpec(loss.shape, lambda i: (0, 0)),
+        ],
+        out_specs=[
+            pl.BlockSpec((1, part, point.shape[2]), lambda i: (i // 2, i % 2, 0)),
+            pl.BlockSpec((rows, embed), lambda i: (i, 0)),
+            pl.BlockSpec(loss.shape, lambda i: (0, 0)),
+        ],
+        out_shape=[
+            jax.ShapeDtypeStruct(point.shape, jnp.float32),
+            jax.ShapeDtypeStruct((2 * width, embed), jnp.float32),
+            jax.ShapeDtypeStruct(loss.shape, jnp.float32),
+        ],
+    )(point, head, loss)
 
 
 def local(
@@ -704,13 +742,8 @@
         n_neg, n_rep, (n0, m0, d0, n1, act1, inverse), upstream, kernels, gains, weights,
         point1, head,
     )
-    return (
-        loss,
-        depth,
-        gain,
-        point.astype(jnp.float32),
-        head.reshape(head_weight.shape).astype(jnp.float32),
-    )
+    point, head, loss = run_widen(point, head, loss)
+    return loss, depth, gain, point, head
 
 
 def solution(mesh):

time: 120 us -> 111 us (0.925)
  other arithmetic: 5.96 us -> 1.35 us
  Pallas kernels: 108 us -> 105 us
    pallas_call x1, Pallas kernels: 30.6 us -> 24.6 us  [run_forward(): pl.pallas_call(functools.partial(forward_kernel, goal_steps), grid_spec=p...]
    convert_element_type x2 -> x0, other arithmetic: 4.61 us -> none  [the longest x1 2.83 us: local(): point.astype(jnp.float32)]
    pallas_call x0 -> x1, Pallas kernels: none -> 3.66 us  [run_widen(): pl.pallas_call(widen_kernel, grid=(4,), in_specs=[pl.BlockSpec((1, part,...]
    unnamed x6 -> x3, local copies, waits for them, and re-layouts: 4.41 us -> 3.9 us
where the time goes in v3:
time: 111 us
  Pallas kernels  105 us (95%)
  local copies, waits for them, and re-layouts  3.9 us (4%)
  other arithmetic  1.35 us (1%)
    pallas_call x1, Pallas kernels, run_lower(): pl.pallas_call(functools.partial(lower_kernel, n_neg, n_rep, steps), grid...  53.1 us
    pallas_call x1, Pallas kernels, run_forward(): pl.pallas_call(functools.partial(forward_kernel, goal_steps), grid_spec=p...  24.6 us
    pallas_call x1, Pallas kernels, run_upper(): pl.pallas_call(upper_kernel, grid_spec=pltpu.PrefetchScalarGridSpec(num_s...  12.2 us
    pallas_call x1, Pallas kernels, run_contrast(): pl.pallas_call(functools.partial(contrast_kernel, n_neg, goal_count), out...  11.3 us
    unnamed x3, local copies, waits for them, and re-layouts  3.9 us
    pallas_call x1, Pallas kernels, run_widen(): pl.pallas_call(widen_kernel, grid=(4,), in_specs=[pl.BlockSpec((1, part,...  3.66 us

profile of v3, /device:TPU:1, one launch (start us, length us, event | category | flops | bytes accessed | tf_op | source)
XLA Modules:
  0.0 110.7 jit_solution(16237196702274225128)
XLA Ops:
  0.6 1.3 %convert_reduce_fusion.lens_ref = s32[40]{0:T(128)} fusion(s32[32,128]{1,0:T(8,128)} %bitcast.6, s32[8,128]{1,0:T(8,128)} %bitcast.7), kind=kLoop, calls=%fused_computation.1 | loop fusion | flops 20440 | bytes 20640 | tf_op jit(solution)/shard_map/reduce_sum | solution.py:735
  2.0 1.3 %copy.14.kern_ref = f32[2,3,512]{2,1,0:T(4,128)} copy(f32[2,3,512]{2,0,1:T(2,128)} %param.14) | data formatting | bytes 24576 | tf_op args[5]
  3.3 24.6 %shard_map.128 = (bf16[40,128,512]{2,1,0:T(8,128)(2,1)}, bf16[40,128,512]{2,1,0:T(8,128)(2,1)}, bf16[40,128,512]{2,1,0:T(8,128)(2,1)}, bf16[40,128,512]{2,1,0:T(...) custom-call(s32[40]{0:T(128)} %convert_reduce_fusion.lens_ref, ...), custom_call_target="tpu_custom_call" | custom-call | tf_op jit(solution)/shard_map/pallas_call | solution.py:107
  27.9 11.3 %shard_map.129 = (f32[1,8]{1,0:T(1,128)}, f32[10,8,512]{2,1,0:T(8,128)}, bf16[2,256,256]{2,1,0:T(8,128)(2,1)}) custom-call(f32[10,8,512]{2,1,0:T(8,128)} %get-tuple-element.32.pooled_ref, bf16[512,256]{1,0:T(8,128)(2,1)} %head_ref.1, s32[1,64]{1,0:T(1,128)} %positive_ref.1), custom_call_target="tpu_custom_call" | custom-call | tf_op jit(solution)/shard_map/pallas_call | solution.py:253
  39.1 12.2 %shard_map.130 = (bf16[40,128,512]{2,1,0:T(8,128)(2,1)}, f32[10,8,512]{2,1,0:T(8,128)}, bf16[2,512,256]{2,1,0:T(8,128)(2,1)}) custom-call(s32[40]{0:T(128)} %convert_reduce_fusion.lens_ref, bf16[40,128,512]{2,1,0:T(8,128)(2,1)} %get-tuple-element.30.m_ref, bf16[40,128,512]{2,1,0:T(8,128)(2,1)} %get-tuple-element.31.d_ref, f32[10,8,512]{2,1,0:T(8,128)} %get-tuple-element.33.up_ref), custom_call_target="tpu_custom_call" | custom-call | tf_op jit(solution)/shard_map/pallas_call | solution.py:308
  51.3 53.1 %shard_map.131 = (bf16[2,512,512]{2,1,0:T(8,128)(2,1)}, bf16[2,256,256]{2,1,0:T(8,128)(2,1)}, f32[2,3,512]{2,1,0:T(4,128)}, f32[2,512]{1,0:T(2,128)}) custom-call(bf16[40,128,512]{2,1,0:T(8,128)(2,1)} %get-tuple-element.26.n0_ref, bf16[40,128,512]{2,1,0:T(8,128)(2,1)} %get-tuple-element.27.m0_ref, bf16[40,128,512]{2,1,0:T(8,128)(2,1)} %get-tuple-element.28.d0_ref, ...), custom_call_target="tpu_custom_call" | custom-call | tf_op jit(solution)/shard_map/pallas_call | solution.py:650
  104.5 1.3 %copy.16 = f32[2,3,512]{2,0,1:T(2,128)} copy(f32[2,3,512]{2,1,0:T(4,128)} %get-tuple-element.48) | data formatting | bytes 24576
  105.8 3.7 %shard_map.132 = (f32[2,512,512]{2,1,0:T(8,128)}, f32[512,256]{1,0:T(8,128)}, f32[1,8]{1,0:T(1,128)}) custom-call(bf16[2,512,512]{2,1,0:T(8,128)(2,1)} %get-tuple-element.39.point_ref, bf16[2,256,256]{2,1,0:T(8,128)(2,1)} %get-tuple-element.40.head_ref, f32[1,8]{1,0:T(1,128)} %get-tuple-element.41.loss_ref), custom_call_target="tpu_custom_call" | custom-call | tf_op jit(solution)/shard_map/pallas_call | solution.py:697
  109.5 1.3 %copy.18 = f32[2,512]{1,0:T(2,128)} copy(f32[2,512]{1,0:T(2,128)} %get-tuple-element.59) | data formatting | bytes 8192

commit v4 on v3

--- a/solution.py
+++ b/solution.py
@@ -13,6 +13,7 @@
 GELU_C = 0.7978845608028654
 GELU_A = 0.044715
 SEQS = 4
+GROUPS = 2
 MESH = pl.DeviceIdType.MESH
 VMEM_LIMIT = 56 * 1024 * 1024
 
@@ -281,10 +282,15 @@
     def _():
         sum_ref[...] = jnp.zeros_like(sum_ref)
 
-    rows = up_ref[0] / length_column(lens_ref, step)
-    scaled_ref[...] = rows[None]
-    mask = length_mask(lens_ref, step, length)
-    upstream = (jnp.stack([rows[s : s + 1] for s in range(SEQS)]) * mask).astype(jnp.bfloat16)
+    rows, mask = [], []
+    for j in range(GROUPS):
+        part = step * GROUPS + j
+        rows.append(up_ref[j] / length_column(lens_ref, part))
+        scaled_ref[j] = rows[j]
+        mask.append(length_mask(lens_ref, part, length))
+    mask = jnp.concatenate(mask, axis=0)
+    spread = jnp.stack([row[s : s + 1] for row in rows for s in range(SEQS)])
+    upstream = (spread * mask).astype(jnp.bfloat16)
     act_grad = upstream * d_ref[...]
     act_ref[...] = act_grad
     sum_ref[...] += lax.dot_general(
@@ -302,9 +308,10 @@
 
 def run_upper(lens, mixed, slope, pooled_grad):
     total, length, width = mixed.shape
-    steps = total // SEQS
-    block = pl.BlockSpec((SEQS, length, width), lambda i, lens: (i, 0, 0))
-    rows = pl.BlockSpec((1, 8, width), lambda i, lens: (i, 0, 0))
+    steps = total // (GROUPS * SEQS)
+    assert total % (GROUPS * SEQS) == 0
+    block = pl.BlockSpec((GROUPS * SEQS, length, width), lambda i, lens: (i, 0, 0))
+    rows = pl.BlockSpec((GROUPS, 8, width), lambda i, lens: (i, 0, 0))
     return pl.pallas_call(
         upper_kernel,
         grid_spec=pltpu.PrefetchScalarGridSpec(

time: 111 us -> 110 us (level)
  Pallas kernels: 105 us -> 103 us
    pallas_call x1, Pallas kernels: 12.2 us -> 10.7 us  [run_upper(): pl.pallas_call(upper_kernel, grid_spec=pltpu.PrefetchScalarGridSpec(num_s...]
where the time goes in v4:
time: 110 us; the launch traced here: 109 us
  Pallas kernels  103 us (94%)
  local copies, waits for them, and re-layouts  3.9 us (4%)
  other arithmetic  1.35 us (1%)
    pallas_call x1, Pallas kernels, run_lower(): pl.pallas_call(functools.partial(lower_kernel, n_neg, n_rep, steps), grid...  53.1 us
    pallas_call x1, Pallas kernels, run_forward(): pl.pallas_call(functools.partial(forward_kernel, goal_steps), grid_spec=p...  24.6 us
    pallas_call x1, Pallas kernels, run_contrast(): pl.pallas_call(functools.partial(contrast_kernel, n_neg, goal_count), out...  11.3 us
    pallas_call x1, Pallas kernels, run_upper(): pl.pallas_call(upper_kernel, grid_spec=pltpu.PrefetchScalarGridSpec(num_s...  10.7 us
    unnamed x3, local copies, waits for them, and re-layouts  3.9 us
    pallas_call x1, Pallas kernels, run_widen(): pl.pallas_call(widen_kernel, grid=(4,), in_specs=[pl.BlockSpec((1, part,...  3.66 us

profile of v4, /device:TPU:1, one launch (start us, length us, event | category | flops | bytes accessed | tf_op | source)
XLA Modules:
  0.0 109.2 jit_solution(2371326400995426456)
XLA Ops:
  0.6 1.3 %convert_reduce_fusion.lens_ref = s32[40]{0:T(128)} fusion(s32[32,128]{1,0:T(8,128)} %bitcast.6, s32[8,128]{1,0:T(8,128)} %bitcast.7), kind=kLoop, calls=%fused_computation.1 | loop fusion | flops 20440 | bytes 20640 | tf_op jit(solution)/shard_map/reduce_sum | solution.py:742
  2.0 1.3 %copy.14.kern_ref = f32[2,3,512]{2,1,0:T(4,128)} copy(f32[2,3,512]{2,0,1:T(2,128)} %param.14) | data formatting | bytes 24576 | tf_op args[5]
  3.3 24.6 %shard_map.128 = (bf16[40,128,512]{2,1,0:T(8,128)(2,1)}, bf16[40,128,512]{2,1,0:T(8,128)(2,1)}, bf16[40,128,512]{2,1,0:T(8,128)(2,1)}, bf16[40,128,512]{2,1,0:T(...) custom-call(s32[40]{0:T(128)} %convert_reduce_fusion.lens_ref, ...), custom_call_target="tpu_custom_call" | custom-call | tf_op jit(solution)/shard_map/pallas_call | solution.py:108
  27.9 11.3 %shard_map.129 = (f32[1,8]{1,0:T(1,128)}, f32[10,8,512]{2,1,0:T(8,128)}, bf16[2,256,256]{2,1,0:T(8,128)(2,1)}) custom-call(f32[10,8,512]{2,1,0:T(8,128)} %get-tuple-element.32.pooled_ref, bf16[512,256]{1,0:T(8,128)(2,1)} %head_ref.1, s32[1,64]{1,0:T(1,128)} %positive_ref.1), custom_call_target="tpu_custom_call" | custom-call | tf_op jit(solution)/shard_map/pallas_call | solution.py:254
  39.1 10.7 %shard_map.130 = (bf16[40,128,512]{2,1,0:T(8,128)(2,1)}, f32[10,8,512]{2,1,0:T(8,128)}, bf16[2,512,256]{2,1,0:T(8,128)(2,1)}) custom-call(s32[40]{0:T(128)} %convert_reduce_fusion.lens_ref, bf16[40,128,512]{2,1,0:T(8,128)(2,1)} %get-tuple-element.30.m_ref, bf16[40,128,512]{2,1,0:T(8,128)(2,1)} %get-tuple-element.31.d_ref, f32[10,8,512]{2,1,0:T(8,128)} %get-tuple-element.33.up_ref), custom_call_target="tpu_custom_call" | custom-call | tf_op jit(solution)/shard_map/pallas_call | solution.py:315
  49.8 53.1 %shard_map.131 = (bf16[2,512,512]{2,1,0:T(8,128)(2,1)}, bf16[2,256,256]{2,1,0:T(8,128)(2,1)}, f32[2,3,512]{2,1,0:T(4,128)}, f32[2,512]{1,0:T(2,128)}) custom-call(bf16[40,128,512]{2,1,0:T(8,128)(2,1)} %get-tuple-element.26.n0_ref, bf16[40,128,512]{2,1,0:T(8,128)(2,1)} %get-tuple-element.27.m0_ref, bf16[40,128,512]{2,1,0:T(8,128)(2,1)} %get-tuple-element.28.d0_ref, ...), custom_call_target="tpu_custom_call" | custom-call | tf_op jit(solution)/shard_map/pallas_call | solution.py:657
  102.9 1.3 %copy.16 = f32[2,3,512]{2,0,1:T(2,128)} copy(f32[2,3,512]{2,1,0:T(4,128)} %get-tuple-element.48) | data formatting | bytes 24576
  104.2 3.7 %shard_map.132 = (f32[2,512,512]{2,1,0:T(8,128)}, f32[512,256]{1,0:T(8,128)}, f32[1,8]{1,0:T(1,128)}) custom-call(bf16[2,512,512]{2,1,0:T(8,128)(2,1)} %get-tuple-element.39.point_ref, bf16[2,256,256]{2,1,0:T(8,128)(2,1)} %get-tuple-element.40.head_ref, f32[1,8]{1,0:T(1,128)} %get-tuple-element.41.loss_ref), custom_call_target="tpu_custom_call" | custom-call | tf_op jit(solution)/shard_map/pallas_call | solution.py:704
  107.9 1.3 %copy.18 = f32[2,512]{1,0:T(2,128)} copy(f32[2,512]{1,0:T(2,128)} %get-tuple-element.59) | data formatting | bytes 8192
